TPU v7x, 512 devices: a whole 4x8x8 slice. The times are simulated.
512 devices in a mesh: dp: 16 (over x, y_lo, core), ctx: 32 (over z, y_hi).
Axes of the slice: x: 4, y: 8 (y_hi: 4, y_lo: 2; y = y_hi * 2 + y_lo), z: 8, core: 2. Of those that a mesh axis runs over, the one named last changes fastest.
Arguments:
- inputs: bfloat16 [16, 8192, 256], P('dp', 'ctx'), may hold values from -6 to 6
- out_grads: bfloat16 [16, 8192, 256], P('dp', 'ctx'), may hold values from -0.015625 to 0.015625
Outputs:
- filter_grad: float32 [8192, 256], P('ctx')
All inputs are finite; a program needn't handle non-finite values.
Results may differ from a plain program's by a relative error of at most 0.0095.
Values may be sent and summed in bfloat16 or wider, within the bound.
No kernel may reach another device: no remote copies, remote signals or barrier semaphores. Data moves between devices by JAX's collectives and lax.ppermute only.
A program may use at most 64 MiB of HBM per device.

v0:
```python
import math

import jax
import jax.numpy as jnp
from jax import lax
from jax.sharding import PartitionSpec as P


def from_behind(block, axis, distance):
    devices = range(lax.axis_size(axis))
    route = [(i - distance, i) for i in devices if i - distance in devices]
    return lax.ppermute(block, axis, route)


def make_tables(blk):
    span = 2 * blk
    freq = jnp.arange(blk, dtype=jnp.int32)[:, None]
    taps = jnp.arange(blk, dtype=jnp.int32)[None, :]
    angle = (freq * taps % span).astype(jnp.float32) * (2.0 * math.pi / span)
    signs = (1 - 2 * (taps % 2)).astype(jnp.float32)
    sine_rows = jnp.where(freq == 0, signs, jnp.sin(angle))
    forward = jnp.concatenate([jnp.cos(angle), sine_rows], axis=0).astype(jnp.bfloat16)
    rows = jnp.arange(span, dtype=jnp.int32)[:, None]
    cols = jnp.arange(blk, dtype=jnp.int32)[None, :]
    angle_back = (rows * cols % span).astype(jnp.float32) * (2.0 * math.pi / span)
    weight = jnp.where(cols == 0, 1.0, 2.0).astype(jnp.float32) / span
    cos_part = weight * jnp.cos(angle_back)
    row_signs = (1 - 2 * (rows % 2)).astype(jnp.float32) / span
    sin_part = jnp.where(cols == 0, row_signs, -weight * jnp.sin(angle_back))
    inverse = jnp.concatenate([cos_part, sin_part], axis=1)
    return (forward, inverse)


def pair_product(grad_spec, in_spec, blk):
    left = grad_spec.astype(jnp.float32)
    right = in_spec.astype(jnp.float32)
    cos_a, sin_a = (left[..., :blk, :], left[..., blk:, :])
    cos_b, sin_b = (right[..., :blk, :], right[..., blk:, :])
    first = (jnp.arange(blk) == 0)[:, None]
    both = sin_a * sin_b
    real = cos_a * cos_b + jnp.where(first, 0.0, both)
    imag = jnp.where(first, both, cos_a * sin_b - sin_a * cos_b)
    return jnp.concatenate([real, imag], axis=-2)


def cycle_correlation(inputs, out_grads, inverse, spectrum, nblk):
    seqs, blk, chans = inputs.shape
    span = 2 * blk
    whole_in = lax.all_gather(inputs, "ctx", axis=1, tiled=True)

    def input_spectrum(index):
        return spectrum(lax.dynamic_slice_in_dim(whole_in, index * blk, blk, 1))

    following = from_behind(out_grads, "ctx", -1)
    window = jnp.concatenate([out_grads, following], axis=1)
    totals = jnp.zeros((seqs, span, chans), jnp.float32)

    def accumulate(step, window, totals):
        running = totals
        for half in range(2):
            grads = window[:, half * blk : (half + 1) * blk]
            running = running + pair_product(spectrum(grads), input_spectrum(2 * step + half), blk)
        return running

    def advance(step, carry):
        window, totals = carry
        totals = accumulate(step, window, totals)
        window = from_behind(window, "ctx", -2)
        return (window, totals)

    window, totals = lax.fori_loop(0, nblk // 2 - 1, advance, (window, totals))
    totals = accumulate(nblk // 2 - 1, window, totals)
    summed = jnp.sum(totals, axis=0)
    return jnp.dot(
        inverse, summed, precision=lax.Precision.HIGHEST, preferred_element_type=jnp.float32
    )


def on_device(inputs, out_grads):
    seqs, blk, chans = inputs.shape
    nblk = lax.axis_size("ctx")
    forward, inverse = make_tables(blk)

    def spectrum(block):
        return jnp.einsum("ft,stc->sfc", forward, block, preferred_element_type=jnp.float32).astype(
            jnp.bfloat16
        )

    correlation = cycle_correlation(inputs, out_grads, inverse, spectrum, nblk)
    later = from_behind(correlation[blk:], "ctx", -1)
    result = correlation[:blk] + later
    result = lax.psum(result, "dp")
    return result


def solution(mesh):
    in_specs = (P("dp", "ctx", None), P("dp", "ctx", None))
    out_specs = P("ctx", None)
    return jax.shard_map(
        on_device, mesh=mesh, in_specs=in_specs, out_specs=out_specs, check_vma=False
    )
```

profile of v0, /device:TPU:1, one launch (start us, length us, event | category | flops | bytes accessed | tf_op | source)
XLA Modules:
  0.0 540.3 jit_solution(7906073943537977880)
XLA Ops:
  9.7 2.7 cosine_multiply_fusion
  12.4 2.7 multiply_select_fusion
  18.1 98.6 %all-gather.2.cloned.1.call-done = bf16[1,8192,256]{2,1,0:T(8,128)(2,1)} async-done(((bf16[1,256,256]{2,1,0:T(8,128)(2,1)}), bf16[1,8192,256]{2,1,0:T(8,128)(2,1)}) %all-gather.2.cloned.1.call-update) | async-done | bytes 4194320 | tf_op jit(solution)/shard_map/all_gather | solution.py:49
  116.7 209.0 %while.18 = (s32[]{:T(128)}, bf16[1,512,256]{2,1,0:T(8,128)(2,1)S(1)}, f32[1,512,256]{1,2,0:T(8,128)}, bf16[512,256]{1,0:T(8,128)(2,1)S(1)}, bf16[1,8192,256]{2,...) while((s32[]{:T(128)}, ...), condition=%wide.region_1.2_spmd.clone, body=%wide.region_0.1_spmd.clone.sunk | while | flops 271188224 | bytes 10486555 | solution.py:71
  122.0 5.8 %collective-permute-done = bf16[1,512,256]{2,1,0:T(8,128)(2,1)S(1)} collective-permute-done((bf16[1,512,256]{2,1,0:T(8,128)(2,1)S(1)}, bf16[1,512,256]{2,1,0:T(8,128)(2,1)S(1)}, u32[]{:S(2)}, u32[]{:S(2)}) %collective-permute-start) | collective-permute-done | bytes 262176 | tf_op jit(solution)/shard_map/while/body/eval_jaxpr/ppermute | solution.py:12
  132.2 2.0 fusion.102
  134.2 4.6 collective-permute-done
  143.3 2.0 fusion.102
  145.3 5.1 collective-permute-done
  154.8 2.0 fusion.102
  156.8 6.3 %collective-permute-done = bf16[1,512,256]{2,1,0:T(8,128)(2,1)S(1)} collective-permute-done((bf16[1,512,256]{2,1,0:T(8,128)(2,1)S(1)}, bf16[1,512,256]{2,1,0:T(8,128)(2,1)S(1)}, u32[]{:S(2)}, u32[]{:S(2)}) %collective-permute-start) | collective-permute-done | bytes 262176 | tf_op jit(solution)/shard_map/while/body/eval_jaxpr/ppermute | solution.py:12
  167.5 2.0 fusion.102
  169.5 8.6 %collective-permute-done = bf16[1,512,256]{2,1,0:T(8,128)(2,1)S(1)} collective-permute-done((bf16[1,512,256]{2,1,0:T(8,128)(2,1)S(1)}, bf16[1,512,256]{2,1,0:T(8,128)(2,1)S(1)}, u32[]{:S(2)}, u32[]{:S(2)}) %collective-permute-start) | collective-permute-done | bytes 262176 | tf_op jit(solution)/shard_map/while/body/eval_jaxpr/ppermute | solution.py:12
  184.5 6.8 %collective-permute-done = bf16[1,512,256]{2,1,0:T(8,128)(2,1)S(1)} collective-permute-done((bf16[1,512,256]{2,1,0:T(8,128)(2,1)S(1)}, bf16[1,512,256]{2,1,0:T(8,128)(2,1)S(1)}, u32[]{:S(2)}, u32[]{:S(2)}) %collective-permute-start) | collective-permute-done | bytes 262176 | tf_op jit(solution)/shard_map/while/body/eval_jaxpr/ppermute | solution.py:12
  195.7 2.0 fusion.102
  197.7 6.1 %collective-permute-done = bf16[1,512,256]{2,1,0:T(8,128)(2,1)S(1)} collective-permute-done((bf16[1,512,256]{2,1,0:T(8,128)(2,1)S(1)}, bf16[1,512,256]{2,1,0:T(8,128)(2,1)S(1)}, u32[]{:S(2)}, u32[]{:S(2)}) %collective-permute-start) | collective-permute-done | bytes 262176 | tf_op jit(solution)/shard_map/while/body/eval_jaxpr/ppermute | solution.py:12
  208.1 2.0 fusion.102
  210.1 15.3 %collective-permute-done = bf16[1,512,256]{2,1,0:T(8,128)(2,1)S(1)} collective-permute-done((bf16[1,512,256]{2,1,0:T(8,128)(2,1)S(1)}, bf16[1,512,256]{2,1,0:T(8,128)(2,1)S(1)}, u32[]{:S(2)}, u32[]{:S(2)}) %collective-permute-start) | collective-permute-done | bytes 262176 | tf_op jit(solution)/shard_map/while/body/eval_jaxpr/ppermute | solution.py:12
  229.8 2.0 fusion.102
  231.8 4.6 collective-permute-done
  242.9 8.5 %collective-permute-done = bf16[1,512,256]{2,1,0:T(8,128)(2,1)S(1)} collective-permute-done((bf16[1,512,256]{2,1,0:T(8,128)(2,1)S(1)}, bf16[1,512,256]{2,1,0:T(8,128)(2,1)S(1)}, u32[]{:S(2)}, u32[]{:S(2)}) %collective-permute-start) | collective-permute-done | bytes 262176 | tf_op jit(solution)/shard_map/while/body/eval_jaxpr/ppermute | solution.py:12
  255.7 2.0 fusion.102
  257.7 10.7 %collective-permute-done = bf16[1,512,256]{2,1,0:T(8,128)(2,1)S(1)} collective-permute-done((bf16[1,512,256]{2,1,0:T(8,128)(2,1)S(1)}, bf16[1,512,256]{2,1,0:T(8,128)(2,1)S(1)}, u32[]{:S(2)}, u32[]{:S(2)}) %collective-permute-start) | collective-permute-done | bytes 262176 | tf_op jit(solution)/shard_map/while/body/eval_jaxpr/ppermute | solution.py:12
  272.9 2.0 fusion.102
  274.9 11.2 %collective-permute-done = bf16[1,512,256]{2,1,0:T(8,128)(2,1)S(1)} collective-permute-done((bf16[1,512,256]{2,1,0:T(8,128)(2,1)S(1)}, bf16[1,512,256]{2,1,0:T(8,128)(2,1)S(1)}, u32[]{:S(2)}, u32[]{:S(2)}) %collective-permute-start) | collective-permute-done | bytes 262176 | tf_op jit(solution)/shard_map/while/body/eval_jaxpr/ppermute | solution.py:12
  292.5 8.5 %collective-permute-done = bf16[1,512,256]{2,1,0:T(8,128)(2,1)S(1)} collective-permute-done((bf16[1,512,256]{2,1,0:T(8,128)(2,1)S(1)}, bf16[1,512,256]{2,1,0:T(8,128)(2,1)S(1)}, u32[]{:S(2)}, u32[]{:S(2)}) %collective-permute-start) | collective-permute-done | bytes 262176 | tf_op jit(solution)/shard_map/while/body/eval_jaxpr/ppermute | solution.py:12
  305.4 2.0 fusion.102
  307.4 6.6 %collective-permute-done = bf16[1,512,256]{2,1,0:T(8,128)(2,1)S(1)} collective-permute-done((bf16[1,512,256]{2,1,0:T(8,128)(2,1)S(1)}, bf16[1,512,256]{2,1,0:T(8,128)(2,1)S(1)}, u32[]{:S(2)}, u32[]{:S(2)}) %collective-permute-start) | collective-permute-done | bytes 262176 | tf_op jit(solution)/shard_map/while/body/eval_jaxpr/ppermute | solution.py:12
  318.4 2.0 fusion.102
  320.4 5.3 collective-permute-done
  333.2 28.2 %collective-permute-done.2 = f32[256,256]{1,0:T(8,128)S(1)} collective-permute-done((f32[256,256]{1,0:T(8,128)S(1)}, f32[256,256]{1,0:T(8,128)S(1)}, u32[]{:S(2)}, u32[]{:S(2)}) %collective-permute-start.2) | collective-permute-done | bytes 262176 | tf_op jit(solution)/shard_map/ppermute | solution.py:12
  362.1 169.7 %all-reduce.2.cloned.1.call-done = f32[256,256]{1,0:T(8,128)} async-done(((f32[256,256]{1,0:T(8,128)}), f32[256,256]{1,0:T(8,128)}) %all-reduce.2.cloned.1.call-update) | async-done | bytes 262160 | tf_op jit(solution)/shard_map/psum | solution.py:92
  (158 shorter events, 87.7 us)
Async XLA Ops:
  6.5 110.1 %all-gather.2.cloned.1.call-start = ((), (), s32[]{:S(2)}) async-start(), calls=%async_computation | async-start | bytes 4325376 | tf_op jit(solution)/shard_map/all_gather | solution.py:49
  7.3 524.6 %all-reduce.2.cloned.1.call-start = ((), (), s32[]{:S(2)}) async-start(), calls=%async_computation.1 | async-start | bytes 524288 | tf_op jit(solution)/shard_map/psum | solution.py:92
  7.3 9.9 %collective-permute-start.1 = (bf16[1,256,256]{2,1,0:T(8,128)(2,1)}, bf16[1,256,256]{2,1,0:T(8,128)(2,1)S(1)}, u32[]{:S(2)}, u32[]{:S(2)}) collective-permute-start(bf16[1,256,256]{2,1,0:T(8,128)(2,1)} %param.5), channel_id=1, source_target_pairs={{1,0},{2,1},{3,2},{4,3},{5,4},{6,5},{7,6},{8,7},{9,8},{10,9},{11,1... | collective-permute-start | bytes 393224 | tf_op jit(solution)/shard_map/ppermute | solution.py:12
  16.1 0.7 copy-start.1
  116.7 11.1 %collective-permute-start = (bf16[1,512,256]{2,1,0:T(8,128)(2,1)S(1)}, bf16[1,512,256]{2,1,0:T(8,128)(2,1)S(1)}, u32[]{:S(2)}, u32[]{:S(2)}) collective-permute-start(bf16[1,512,256]{2,1,0:T(8,128)(2,1)S(1)} %copy.11), channel_id=1, source_target_pairs={{2,0},{3,1},{4,2},{5,3},{6,4},{7,5},{8,6},{9,7},{10,8},{11,9},{12,... | collective-permute-start | bytes 786440 | tf_op jit(solution)/shard_map/while/body/eval_jaxpr/ppermute | solution.py:12
  127.9 11.0 %collective-permute-start = (bf16[1,512,256]{2,1,0:T(8,128)(2,1)S(1)}, bf16[1,512,256]{2,1,0:T(8,128)(2,1)S(1)}, u32[]{:S(2)}, u32[]{:S(2)}) collective-permute-start(bf16[1,512,256]{2,1,0:T(8,128)(2,1)S(1)} %copy.11), channel_id=1, source_target_pairs={{2,0},{3,1},{4,2},{5,3},{6,4},{7,5},{8,6},{9,7},{10,8},{11,9},{12,... | collective-permute-start | bytes 786440 | tf_op jit(solution)/shard_map/while/body/eval_jaxpr/ppermute | solution.py:12
  138.9 11.5 %collective-permute-start = (bf16[1,512,256]{2,1,0:T(8,128)(2,1)S(1)}, bf16[1,512,256]{2,1,0:T(8,128)(2,1)S(1)}, u32[]{:S(2)}, u32[]{:S(2)}) collective-permute-start(bf16[1,512,256]{2,1,0:T(8,128)(2,1)S(1)} %copy.11), channel_id=1, source_target_pairs={{2,0},{3,1},{4,2},{5,3},{6,4},{7,5},{8,6},{9,7},{10,8},{11,9},{12,... | collective-permute-start | bytes 786440 | tf_op jit(solution)/shard_map/while/body/eval_jaxpr/ppermute | solution.py:12
  150.4 12.7 %collective-permute-start = (bf16[1,512,256]{2,1,0:T(8,128)(2,1)S(1)}, bf16[1,512,256]{2,1,0:T(8,128)(2,1)S(1)}, u32[]{:S(2)}, u32[]{:S(2)}) collective-permute-start(bf16[1,512,256]{2,1,0:T(8,128)(2,1)S(1)} %copy.11), channel_id=1, source_target_pairs={{2,0},{3,1},{4,2},{5,3},{6,4},{7,5},{8,6},{9,7},{10,8},{11,9},{12,... | collective-permute-start | bytes 786440 | tf_op jit(solution)/shard_map/while/body/eval_jaxpr/ppermute | solution.py:12
  163.1 15.0 %collective-permute-start = (bf16[1,512,256]{2,1,0:T(8,128)(2,1)S(1)}, bf16[1,512,256]{2,1,0:T(8,128)(2,1)S(1)}, u32[]{:S(2)}, u32[]{:S(2)}) collective-permute-start(bf16[1,512,256]{2,1,0:T(8,128)(2,1)S(1)} %copy.11), channel_id=1, source_target_pairs={{2,0},{3,1},{4,2},{5,3},{6,4},{7,5},{8,6},{9,7},{10,8},{11,9},{12,... | collective-permute-start | bytes 786440 | tf_op jit(solution)/shard_map/while/body/eval_jaxpr/ppermute | solution.py:12
  178.1 13.2 %collective-permute-start = (bf16[1,512,256]{2,1,0:T(8,128)(2,1)S(1)}, bf16[1,512,256]{2,1,0:T(8,128)(2,1)S(1)}, u32[]{:S(2)}, u32[]{:S(2)}) collective-permute-start(bf16[1,512,256]{2,1,0:T(8,128)(2,1)S(1)} %copy.11), channel_id=1, source_target_pairs={{2,0},{3,1},{4,2},{5,3},{6,4},{7,5},{8,6},{9,7},{10,8},{11,9},{12,... | collective-permute-start | bytes 786440 | tf_op jit(solution)/shard_map/while/body/eval_jaxpr/ppermute | solution.py:12
  191.3 12.4 %collective-permute-start = (bf16[1,512,256]{2,1,0:T(8,128)(2,1)S(1)}, bf16[1,512,256]{2,1,0:T(8,128)(2,1)S(1)}, u32[]{:S(2)}, u32[]{:S(2)}) collective-permute-start(bf16[1,512,256]{2,1,0:T(8,128)(2,1)S(1)} %copy.11), channel_id=1, source_target_pairs={{2,0},{3,1},{4,2},{5,3},{6,4},{7,5},{8,6},{9,7},{10,8},{11,9},{12,... | collective-permute-start | bytes 786440 | tf_op jit(solution)/shard_map/while/body/eval_jaxpr/ppermute | solution.py:12
  203.8 21.7 %collective-permute-start = (bf16[1,512,256]{2,1,0:T(8,128)(2,1)S(1)}, bf16[1,512,256]{2,1,0:T(8,128)(2,1)S(1)}, u32[]{:S(2)}, u32[]{:S(2)}) collective-permute-start(bf16[1,512,256]{2,1,0:T(8,128)(2,1)S(1)} %copy.11), channel_id=1, source_target_pairs={{2,0},{3,1},{4,2},{5,3},{6,4},{7,5},{8,6},{9,7},{10,8},{11,9},{12,... | collective-permute-start | bytes 786440 | tf_op jit(solution)/shard_map/while/body/eval_jaxpr/ppermute | solution.py:12
  225.4 11.0 %collective-permute-start = (bf16[1,512,256]{2,1,0:T(8,128)(2,1)S(1)}, bf16[1,512,256]{2,1,0:T(8,128)(2,1)S(1)}, u32[]{:S(2)}, u32[]{:S(2)}) collective-permute-start(bf16[1,512,256]{2,1,0:T(8,128)(2,1)S(1)} %copy.11), channel_id=1, source_target_pairs={{2,0},{3,1},{4,2},{5,3},{6,4},{7,5},{8,6},{9,7},{10,8},{11,9},{12,... | collective-permute-start | bytes 786440 | tf_op jit(solution)/shard_map/while/body/eval_jaxpr/ppermute | solution.py:12
  236.5 14.8 %collective-permute-start = (bf16[1,512,256]{2,1,0:T(8,128)(2,1)S(1)}, bf16[1,512,256]{2,1,0:T(8,128)(2,1)S(1)}, u32[]{:S(2)}, u32[]{:S(2)}) collective-permute-start(bf16[1,512,256]{2,1,0:T(8,128)(2,1)S(1)} %copy.11), channel_id=1, source_target_pairs={{2,0},{3,1},{4,2},{5,3},{6,4},{7,5},{8,6},{9,7},{10,8},{11,9},{12,... | collective-permute-start | bytes 786440 | tf_op jit(solution)/shard_map/while/body/eval_jaxpr/ppermute | solution.py:12
  251.4 17.1 %collective-permute-start = (bf16[1,512,256]{2,1,0:T(8,128)(2,1)S(1)}, bf16[1,512,256]{2,1,0:T(8,128)(2,1)S(1)}, u32[]{:S(2)}, u32[]{:S(2)}) collective-permute-start(bf16[1,512,256]{2,1,0:T(8,128)(2,1)S(1)} %copy.11), channel_id=1, source_target_pairs={{2,0},{3,1},{4,2},{5,3},{6,4},{7,5},{8,6},{9,7},{10,8},{11,9},{12,... | collective-permute-start | bytes 786440 | tf_op jit(solution)/shard_map/while/body/eval_jaxpr/ppermute | solution.py:12
  268.5 17.6 %collective-permute-start = (bf16[1,512,256]{2,1,0:T(8,128)(2,1)S(1)}, bf16[1,512,256]{2,1,0:T(8,128)(2,1)S(1)}, u32[]{:S(2)}, u32[]{:S(2)}) collective-permute-start(bf16[1,512,256]{2,1,0:T(8,128)(2,1)S(1)} %copy.11), channel_id=1, source_target_pairs={{2,0},{3,1},{4,2},{5,3},{6,4},{7,5},{8,6},{9,7},{10,8},{11,9},{12,... | collective-permute-start | bytes 786440 | tf_op jit(solution)/shard_map/while/body/eval_jaxpr/ppermute | solution.py:12
  286.1 14.9 %collective-permute-start = (bf16[1,512,256]{2,1,0:T(8,128)(2,1)S(1)}, bf16[1,512,256]{2,1,0:T(8,128)(2,1)S(1)}, u32[]{:S(2)}, u32[]{:S(2)}) collective-permute-start(bf16[1,512,256]{2,1,0:T(8,128)(2,1)S(1)} %copy.11), channel_id=1, source_target_pairs={{2,0},{3,1},{4,2},{5,3},{6,4},{7,5},{8,6},{9,7},{10,8},{11,9},{12,... | collective-permute-start | bytes 786440 | tf_op jit(solution)/shard_map/while/body/eval_jaxpr/ppermute | solution.py:12
  301.0 13.0 %collective-permute-start = (bf16[1,512,256]{2,1,0:T(8,128)(2,1)S(1)}, bf16[1,512,256]{2,1,0:T(8,128)(2,1)S(1)}, u32[]{:S(2)}, u32[]{:S(2)}) collective-permute-start(bf16[1,512,256]{2,1,0:T(8,128)(2,1)S(1)} %copy.11), channel_id=1, source_target_pairs={{2,0},{3,1},{4,2},{5,3},{6,4},{7,5},{8,6},{9,7},{10,8},{11,9},{12,... | collective-permute-start | bytes 786440 | tf_op jit(solution)/shard_map/while/body/eval_jaxpr/ppermute | solution.py:12
  314.0 11.6 %collective-permute-start = (bf16[1,512,256]{2,1,0:T(8,128)(2,1)S(1)}, bf16[1,512,256]{2,1,0:T(8,128)(2,1)S(1)}, u32[]{:S(2)}, u32[]{:S(2)}) collective-permute-start(bf16[1,512,256]{2,1,0:T(8,128)(2,1)S(1)} %copy.11), channel_id=1, source_target_pairs={{2,0},{3,1},{4,2},{5,3},{6,4},{7,5},{8,6},{9,7},{10,8},{11,9},{12,... | collective-permute-start | bytes 786440 | tf_op jit(solution)/shard_map/while/body/eval_jaxpr/ppermute | solution.py:12
  325.7 5.1 copy-start
  325.7 5.1 copy-start.2
  325.7 5.1 copy-start.3
  331.9 29.5 %collective-permute-start.2 = (f32[256,256]{1,0:T(8,128)S(1)}, f32[256,256]{1,0:T(8,128)S(1)}, u32[]{:S(2)}, u32[]{:S(2)}) collective-permute-start(f32[256,256]{1,0:T(8,128)S(1)} %slice.175), channel_id=1, source_target_pairs={{1,0},{2,1},{3,2},{4,3},{5,4},{6,5},{7,6},{8,7},{9,8},{10,9},{11,1... | collective-permute-start | bytes 786440 | tf_op jit(solution)/shard_map/ppermute | solution.py:12
Sparse Core Ops, SparseCore 0:
  10.5 106.1 all-gather.1
  362.2 169.5 all-reduce.1
where the time goes:
time: 542 us; the launch traced here: 540 us
  waiting for transfers between devices  412 us (76%)
  matrix products  49 us (9%)
  other arithmetic  40.5 us (7%)
  starting transfers between devices  22 us (4%)
  between operations  13.6 us (3%)
    psum x1, waiting for transfers between devices, on_device(): result = lax.psum(result, 'dp')  170 us
    ppermute x17, waiting for transfers between devices, from_behind(): return lax.ppermute(block, axis, route)  143 us
    all_gather x1, waiting for transfers between devices, cycle_correlation(): whole_in = lax.all_gather(inputs, 'ctx', axis=1, tiled=True)  98.6 us
    dot_general x64, matrix products, spectrum(): jnp.einsum('ft,stc->sfc', forward, block, preferred_element_type=jnp.floa...  47.9 us
    add x15, other arithmetic, accumulate(): running + pair_product(spectrum(grads), input_spectrum(2 * step + half),...  28.9 us
    ppermute x17, starting transfers between devices, from_behind(): return lax.ppermute(block, axis, route)  22 us
  transfers between devices with their start and end apart: 19, of which 19 were waited for; matrix products, arithmetic and copies ran while one was open for 15% of the time, Pallas kernels for 0%

commit v1 on v0

v1 whole, which is shorter than its diff:
```python
import itertools
import math

import jax
import jax.numpy as jnp
import ml_dtypes
import numpy as np
from jax import lax
from jax.experimental import pallas as pl
from jax.experimental.pallas import tpu as pltpu
from jax.sharding import PartitionSpec as P

BLK = 256
NBLK = 32
LANES = 128
PLANE = 128
ROWS = 4
XS = 4
SIZES = {"x": 4, "y_lo": 2, "core": 2, "z": 8, "y_hi": 4}
F32 = jnp.float32
BF16 = jnp.bfloat16
LIMIT = 48 * 1024 * 1024


def groups_over(axes):
    rest = [a for a in SIZES if a not in axes]
    groups = []
    for fixed in itertools.product(*[range(SIZES[a]) for a in rest]):
        group = []
        for moving in itertools.product(*[range(SIZES[a]) for a in axes]):
            place = dict(zip(rest, fixed)) | dict(zip(axes, moving))
            flat = 0
            for a in SIZES:
                flat = flat * SIZES[a] + place[a]
            group.append(flat)
        groups.append(group)
    return groups


PLANE_GROUPS = groups_over(("z", "y_hi", "y_lo", "core"))
X_GROUPS = groups_over(("x",))


def exchange(rows, groups):
    return lax.all_to_all(rows, ("dp", "ctx"), 0, 0, axis_index_groups=groups, tiled=True)


def make_tables():
    span = 2 * BLK
    freq = np.arange(BLK)[:, None]
    taps = np.arange(BLK)[None, :]
    angle = (freq * taps % span) * (2.0 * math.pi / span)
    signs = 1.0 - 2.0 * (taps % 2)
    sines = np.where(freq == 0, signs, np.sin(angle))
    forward = np.concatenate([np.cos(angle), sines], axis=0)
    weight = np.where(freq == 0, 1.0, 2.0) / span
    back = np.concatenate([weight * np.cos(angle), np.where(freq == 0, signs / span, -weight * np.sin(angle))], axis=0)
    back = back.astype(np.float32)
    high = back.astype(ml_dtypes.bfloat16)
    low = (back - high.astype(np.float32)).astype(ml_dtypes.bfloat16)
    return forward.T.astype(ml_dtypes.bfloat16), high, low


def dot(a, b):
    return jnp.dot(a, b, preferred_element_type=F32)


def permutation(source_of):
    row = lax.broadcasted_iota(jnp.int32, (BLK, BLK), 0)
    col = lax.broadcasted_iota(jnp.int32, (BLK, BLK), 1)
    return jnp.where(col == source_of(row), 1.0, 0.0).astype(BF16)


def pack_kernel(in_ref, grad_ref, out_ref):
    turned = [jnp.transpose(in_ref[...].astype(F32)).astype(BF16), jnp.transpose(grad_ref[...].astype(F32)).astype(BF16)]
    perm = permutation(lambda m: (m & 7) * 32 + (m >> 3))
    for part in range(4):
        pieces = []
        for a in range(2):
            for c in range(2):
                for th in range(2):
                    start = c * LANES + part * 32
                    pieces.append(turned[a][start : start + 32, th * LANES : (th + 1) * LANES])
        out_ref[part * BLK : (part + 1) * BLK, :] = dot(perm, jnp.concatenate(pieces, axis=0)).astype(BF16)


def correlate_kernel(rows_ref, forward_ref, high_ref, low_ref, out_ref, xc, xs, xd, gc, gs, zed, ybuf):
    def source(m):
        a, th, j8, r, c = m >> 7, (m >> 6) & 1, (m >> 3) & 7, (m >> 1) & 3, m & 1
        return j8 * 32 + r * 8 + a * 4 + c * 2 + th

    perm = permutation(source)
    blocks = [[], []]
    for part in range(4):
        q = dot(perm, rows_ref[part * BLK : (part + 1) * BLK, :]).astype(BF16)
        for a in range(2):
            at = a * 128
            blocks[a].append(jnp.concatenate([q[at : at + 64], q[at + 64 : at + 128]], axis=1))
    first = lax.broadcasted_iota(jnp.int32, (BLK, LANES), 1) == 0
    forward = forward_ref[...]
    spec_in = dot(jnp.concatenate(blocks[0], axis=0), forward).astype(BF16).astype(F32)
    spec_grad = dot(jnp.concatenate(blocks[1], axis=0), forward).astype(BF16).astype(F32)
    for half in range(2):
        up = slice(half * LANES, (half + 1) * LANES)
        down = slice(BLK + half * LANES, BLK + (half + 1) * LANES)
        cos_in, sin_in = spec_in[:, up], spec_in[:, down]
        xc[half] = cos_in
        if half == 0:
            xs[half] = jnp.where(first, 0.0, sin_in)
            xd[half] = jnp.where(first, -sin_in, cos_in)
        else:
            xs[half] = sin_in
            xd[half] = cos_in
        gc[half] = spec_grad[:, up]
        gs[half] = spec_grad[:, down]

    sign = jnp.where(lax.broadcasted_iota(jnp.int32, (8, LANES), 1) % 2 == 0, 1.0, -1.0)
    width = 4

    def one_half(half, carry):
        def at(ref, j):
            return ref[half, j * 8 : (j + 1) * 8, :]

        after_re = jnp.zeros((8, LANES), F32)
        after_im = jnp.zeros((8, LANES), F32)
        for k0 in reversed(range(0, NBLK, width)):
            re = [None] * width
            im = [None] * width
            for i in range(k0, NBLK):
                g_c, g_s = at(gc, i), at(gs, i)
                for kk in range(width):
                    j = i - k0 - kk
                    if j < 0:
                        continue
                    x_c, x_s, x_d = at(xc, j), at(xs, j), at(xd, j)
                    new_re = g_c * x_c + g_s * x_s
                    new_im = g_c * x_s - g_s * x_d
                    re[kk] = new_re if re[kk] is None else re[kk] + new_re
                    im[kk] = new_im if im[kk] is None else im[kk] + new_im
            for kk in reversed(range(width)):
                k = k0 + kk
                for value, after, where in ((re[kk], after_re, 0), (im[kk], after_im, 1)):
                    total = value + sign * after
                    total = total + pltpu.roll(total, 4, 0)
                    total = total + pltpu.roll(total, 2, 0)
                    zed[where * 2 + half, 2 * k : 2 * k + 2, :] = total[0:2]
                after_re, after_im = re[kk], im[kk]
        return carry

    lax.fori_loop(0, 2, one_half, 0)
    z = jnp.concatenate([zed[n] for n in range(4)], axis=1)
    z_high = z.astype(BF16)
    z_low = (z - z_high.astype(F32)).astype(BF16)
    high = high_ref[...]
    y = dot(z_high, high) + (dot(z_low, high) + dot(z_high, low_ref[...]))
    for lh in range(2):
        ybuf[pl.ds(lh, 64, stride=2), :] = y[:, lh * LANES : (lh + 1) * LANES]
    y = ybuf[...].astype(BF16)
    for n in range(XS):
        out_ref[n * LANES : (n + 1) * LANES, :] = y


def total_kernel(parts_ref, out_ref):
    total = parts_ref[0:LANES].astype(F32)
    for n in range(1, XS):
        total = total + parts_ref[n * LANES : (n + 1) * LANES].astype(F32)
    row = lax.broadcasted_iota(jnp.int32, (512, LANES), 0)
    col = lax.broadcasted_iota(jnp.int32, (512, LANES), 1)
    repeat = jnp.where(col == (row >> 4) * 4 + (row & 3), 1.0, 0.0).astype(BF16)
    out_ref[...] = dot(repeat, total.astype(BF16)).astype(BF16)


def unpack_kernel(rows_ref, out_ref):
    perm = permutation(lambda m: (m & 63) * 4 + (m >> 6))
    halves = [dot(perm, rows_ref[part * BLK : (part + 1) * BLK, :]) for part in range(2)]
    for c in range(2):
        for lh in range(2):
            s = c * 2 + lh
            block = jnp.concatenate([h[s * 64 : (s + 1) * 64] for h in halves], axis=0)
            out_ref[lh * LANES : (lh + 1) * LANES, c * LANES : (c + 1) * LANES] = jnp.transpose(block)


def call(kernel, shape, dtype, count, scratch=()):
    return pl.pallas_call(
        kernel,
        out_shape=jax.ShapeDtypeStruct(shape, dtype),
        in_specs=[pl.BlockSpec(memory_space=pltpu.VMEM)] * count,
        out_specs=pl.BlockSpec(memory_space=pltpu.VMEM),
        scratch_shapes=list(scratch),
        compiler_params=pltpu.CompilerParams(vmem_limit_bytes=LIMIT),
    )


def on_device(inputs, out_grads):
    forward, high, low = make_tables()
    rows = call(pack_kernel, (1024, LANES), BF16, 2)(inputs[0], out_grads[0])
    rows = exchange(rows, PLANE_GROUPS)
    spec = pltpu.VMEM((2, BLK, LANES), F32)
    scratch = [spec] * 5 + [pltpu.VMEM((4, 64, LANES), F32), pltpu.VMEM((LANES, LANES), F32)]
    parts = call(correlate_kernel, (XS * LANES, LANES), BF16, 4, scratch)(rows, forward, high, low)
    parts = exchange(parts, X_GROUPS)
    rows = call(total_kernel, (512, LANES), BF16, 1)(parts)
    rows = exchange(rows, PLANE_GROUPS)
    return call(unpack_kernel, (BLK, BLK), F32, 1)(rows)


def solution(mesh):
    in_specs = (P("dp", "ctx", None), P("dp", "ctx", None))
    out_specs = P("ctx", None)
    return jax.shard_map(on_device, mesh=mesh, in_specs=in_specs, out_specs=out_specs, check_vma=False)
```

time: 542 us -> 67.3 us (0.12)
  waiting for transfers between devices: 412 us -> 0 us
  blocking collectives: 0 us -> 61.4 us
  matrix products: 49 us -> 0 us
  other arithmetic: 40.5 us -> 0 us
  starting transfers between devices: 22 us -> 0 us
  between operations: 13.6 us -> 0.04 us
    psum x1 -> x0, waiting for transfers between devices: 170 us -> none  [on_device(): result = lax.psum(result, 'dp')]
    ppermute x17 -> x0, waiting for transfers between devices: 143 us -> none  [from_behind(): return lax.ppermute(block, axis, route)]
    all_gather x1 -> x0, waiting for transfers between devices: 98.6 us -> none  [cycle_correlation(): whole_in = lax.all_gather(inputs, 'ctx', axis=1, tiled=True)]
    all_to_all x0 -> x3, blocking collectives: none -> 61.4 us  [exchange(): lax.all_to_all(rows, ('dp', 'ctx'), 0, 0, axis_index_groups=groups, tiled...]
    dot_general x65 -> x0, matrix products: 49 us -> none  [the longest x64 47.9 us: spectrum(): jnp.einsum('ft,stc->sfc', forward, block, preferred_element_type=jnp.floa...]
    add x32 -> x0, other arithmetic: 31.9 us -> none  [the longest x15 28.9 us: accumulate(): running + pair_product(spectrum(grads), input_spectrum(2 * step + half),...]
    ppermute x17 -> x0, starting transfers between devices: 22 us -> none  [from_behind(): return lax.ppermute(block, axis, route)]
  transfers between devices with their start and end apart: 19 -> 0, of which waited for: 19 -> 0; matrix products, arithmetic and copies ran while one was open for 15% -> 0% of each run, Pallas kernels for 0% -> 0%
where the time goes in v1:
time: 67.3 us; the launch traced here: 67 us
  blocking collectives  61.4 us (91%)
  Pallas kernels  3.78 us (6%)
  local copies, waits for them, and re-layouts  1.82 us (3%)
    all_to_all x3, blocking collectives, exchange(): lax.all_to_all(rows, ('dp', 'ctx'), 0, 0, axis_index_groups=groups, tiled...  61.4 us
    pallas_call x1, Pallas kernels, on_device(): call(correlate_kernel, (XS * LANES, LANES), BF16, 4, scratch)  2.18 us
    unnamed x10, local copies, waits for them, and re-layouts  1.82 us

profile of v1, /device:TPU:1, one launch (start us, length us, event | category | flops | bytes accessed | tf_op | source)
XLA Modules:
  0.0 67.0 jit_solution(6198102633676382896)
XLA Ops:
  0.0 0.0 copy-start.3
  0.0 0.9 %copy-done.3 = bf16[1,256,256]{2,1,0:T(8,128)(2,1)S(1)} copy-done((bf16[1,256,256]{2,1,0:T(8,128)(2,1)S(1)}, bf16[1,256,256]{2,1,0:T(8,128)(2,1)}, u32[]{:S(2)}) %copy-start.3) | copy-done | bytes 131096
  0.9 0.0 copy-start.4
  0.9 0.9 %copy-done.4 = bf16[1,256,256]{2,1,0:T(8,128)(2,1)S(1)} copy-done((bf16[1,256,256]{2,1,0:T(8,128)(2,1)S(1)}, bf16[1,256,256]{2,1,0:T(8,128)(2,1)}, u32[]{:S(2)}) %copy-start.4) | copy-done | bytes 131096
  1.8 0.0 copy-start.2
  1.8 0.4 shard_map.55
  2.2 0.0 copy-start
  2.2 0.0 copy-start.1
  2.2 33.6 %all_to_all.33 = bf16[128,8,128]{2,1,0:T(8,128)(2,1)S(1)} all-to-all(bf16[128,8,128]{2,1,0:T(8,128)(2,1)S(1)} %bitcast.8), channel_id=1, replica_groups={{0,32,64,96,1,33,65,97,2,34,66,98,3,35,67,99,4,36,68,100,5,37,69,101,6,..., dimensions={0} | all-to-all | bytes 524288 | tf_op jit(solution)/shard_map/all_to_all | solution.py:45
  35.8 0.0 copy-done.2
  35.9 0.0 copy-done
  35.9 0.0 copy-done.1
  35.9 2.2 %shard_map.56 = bf16[512,128]{1,0:T(8,128)(2,1)S(1)} custom-call(bf16[1024,128]{1,0:T(8,128)(2,1)S(1)} %bitcast.9, bf16[256,512]{1,0:T(8,128)(2,1)S(1)} %copy-done.2, bf16[512,256]{1,0:T(8,128)(2,1)S(1)} %copy-done.1, bf16[512,256]{1,0:T(8,128)(2,1)S(1)} %copy-done), custom_call_target="tpu_custom_call" | custom-call | tf_op jit(solution)/shard_map/pallas_call | solution.py:200
  38.0 8.6 %all_to_all.34 = bf16[4,128,128]{2,1,0:T(8,128)(2,1)S(1)} all-to-all(bf16[4,128,128]{2,1,0:T(8,128)(2,1)S(1)} %bitcast.10), channel_id=1, replica_groups={{0,128,256,384},{1,129,257,385},{2,130,258,386},{3,131,259,387},{4,132,..., dimensions={0} | all-to-all | bytes 262144 | tf_op jit(solution)/shard_map/all_to_all | solution.py:45
  46.7 0.2 shard_map.57
  46.9 19.2 %all_to_all.35 = bf16[128,4,128]{2,1,0:T(4,128)(2,1)S(1)} all-to-all(bf16[128,4,128]{2,1,0:T(4,128)(2,1)S(1)} %bitcast.13), channel_id=1, replica_groups={{0,32,64,96,1,33,65,97,2,34,66,98,3,35,67,99,4,36,68,100,5,37,69,101,6,..., dimensions={0} | all-to-all | bytes 262144 | tf_op jit(solution)/shard_map/all_to_all | solution.py:45
  66.0 1.0 %shard_map.58 = f32[256,256]{1,0:T(8,128)} custom-call(bf16[512,128]{1,0:T(8,128)(2,1)S(1)} %bitcast.11), custom_call_target="tpu_custom_call" | custom-call | tf_op jit(solution)/shard_map/pallas_call | solution.py:204
Async XLA Ops:
  0.0 0.9 %copy-start.3 = (bf16[1,256,256]{2,1,0:T(8,128)(2,1)S(1)}, bf16[1,256,256]{2,1,0:T(8,128)(2,1)}, u32[]{:S(2)}) copy-start(bf16[1,256,256]{2,1,0:T(8,128)(2,1)} %param.5) | copy-start | bytes 393220
  0.9 0.9 %copy-start.4 = (bf16[1,256,256]{2,1,0:T(8,128)(2,1)S(1)}, bf16[1,256,256]{2,1,0:T(8,128)(2,1)}, u32[]{:S(2)}) copy-start(bf16[1,256,256]{2,1,0:T(8,128)(2,1)} %param.6) | copy-start | bytes 393220
  1.8 34.0 %copy-start.2 = (bf16[256,512]{1,0:T(8,128)(2,1)S(1)}, bf16[256,512]{1,0:T(8,128)(2,1)}, u32[]{:S(2)}) copy-start(bf16[256,512]{1,0:T(8,128)(2,1)} %constant.6.clone.forward_ref) | copy-start | bytes 786436
  2.2 33.6 %copy-start = (bf16[512,256]{1,0:T(8,128)(2,1)S(1)}, bf16[512,256]{1,0:T(8,128)(2,1)}, u32[]{:S(2)}) copy-start(bf16[512,256]{1,0:T(8,128)(2,1)} %constant.8.clone.low_ref) | copy-start | bytes 786436
  2.2 33.6 %copy-start.1 = (bf16[512,256]{1,0:T(8,128)(2,1)S(1)}, bf16[512,256]{1,0:T(8,128)(2,1)}, u32[]{:S(2)}) copy-start(bf16[512,256]{1,0:T(8,128)(2,1)} %constant.7.clone.high_ref) | copy-start | bytes 786436

commit v2 on v1

v2 whole, which is shorter than its diff:
```python
import itertools
import math

import jax
import jax.numpy as jnp
import ml_dtypes
import numpy as np
from jax import lax
from jax.experimental import pallas as pl
from jax.experimental.pallas import tpu as pltpu
from jax.sharding import PartitionSpec as P

BLK = 256
NBLK = 32
LANES = 128
SIZES = {"x": 4, "y_lo": 2, "core": 2, "z": 8, "y_hi": 4}
F32 = jnp.float32
BF16 = jnp.bfloat16
LIMIT = 48 * 1024 * 1024


def groups_over(axes):
    rest = [a for a in SIZES if a not in axes]
    groups = []
    for fixed in itertools.product(*[range(SIZES[a]) for a in rest]):
        group = []
        for moving in itertools.product(*[range(SIZES[a]) for a in axes]):
            place = dict(zip(rest, fixed)) | dict(zip(axes, moving))
            flat = 0
            for a in SIZES:
                flat = flat * SIZES[a] + place[a]
            group.append(flat)
        groups.append(group)
    return groups


HALF_GROUPS = groups_over(("z", "y_hi", "y_lo"))
SUM_GROUPS = groups_over(("x", "core"))
PLANE_GROUPS = groups_over(("z", "y_hi", "y_lo", "core"))


def exchange(rows, groups):
    return lax.all_to_all(rows, ("dp", "ctx"), 0, 0, axis_index_groups=groups, tiled=True)


def make_tables():
    span = 2 * BLK
    freq = np.arange(BLK)[:, None]
    taps = np.arange(BLK)[None, :]
    angle = (freq * taps % span) * (2.0 * math.pi / span)
    signs = 1.0 - 2.0 * (taps % 2)
    sines = np.where(freq == 0, signs, np.sin(angle))
    forward = np.concatenate([np.cos(angle), sines], axis=0)
    weight = np.where(freq == 0, 1.0, 2.0) / span
    back = np.concatenate([weight * np.cos(angle), np.where(freq == 0, signs / span, -weight * np.sin(angle))], axis=0)
    back = back.astype(np.float32)
    high = back.astype(ml_dtypes.bfloat16)
    low = (back - high.astype(np.float32)).astype(ml_dtypes.bfloat16)
    return forward.T.astype(ml_dtypes.bfloat16), high, low


def dot(a, b):
    return jnp.dot(a, b, preferred_element_type=F32)


def permutation(source_of):
    row = lax.broadcasted_iota(jnp.int32, (BLK, BLK), 0)
    col = lax.broadcasted_iota(jnp.int32, (BLK, BLK), 1)
    return jnp.where(col == source_of(row), 1.0, 0.0).astype(BF16)


def pack_kernel(in_hbm, grad_hbm, out_ref, held, sems):
    copies = [pltpu.make_async_copy(ref, held.at[a], sems.at[a]) for a, ref in enumerate((in_hbm, grad_hbm))]
    for copy in copies:
        copy.start()
    perm = permutation(lambda m: (m & 15) * 16 + (m >> 4))
    turned = []
    for a in range(2):
        copies[a].wait()
        turned.append(jnp.transpose(held[a].astype(F32)).astype(BF16))
    for part in range(4):
        pieces = []
        for a in range(2):
            for c in range(4):
                for th in range(2):
                    start = c * 64 + part * 16
                    pieces.append(turned[a][start : start + 16, th * LANES : (th + 1) * LANES])
        out_ref[part * BLK : (part + 1) * BLK, :] = dot(perm, jnp.concatenate(pieces, axis=0)).astype(BF16)


def correlate_kernel(rows_ref, forward_ref, high_ref, low_ref, out_ref, xa, xb, xc, ga, gb, gc, zed, ybuf):
    def source(m):
        a, th, j8, r, c = m >> 7, (m >> 6) & 1, (m >> 3) & 7, (m >> 2) & 1, m & 3
        return j8 * 32 + r * 16 + a * 8 + c * 2 + th

    perm = permutation(source)
    blocks = [[], []]
    for part in range(4):
        q = dot(perm, rows_ref[part * BLK : (part + 1) * BLK, :]).astype(BF16)
        for a in range(2):
            at = a * 128
            blocks[a].append(jnp.concatenate([q[at : at + 64], q[at + 64 : at + 128]], axis=1))
    first = lax.broadcasted_iota(jnp.int32, (BLK, LANES), 1) == 0
    forward = forward_ref[...]
    spec_in = dot(jnp.concatenate(blocks[0], axis=0), forward).astype(BF16).astype(F32)
    spec_grad = dot(jnp.concatenate(blocks[1], axis=0), forward).astype(BF16).astype(F32)
    for half in range(2):
        up = slice(half * LANES, (half + 1) * LANES)
        down = slice(BLK + half * LANES, BLK + (half + 1) * LANES)
        cos_in, sin_in = spec_in[:, up], spec_in[:, down]
        cos_grad, sin_grad = spec_grad[:, up], spec_grad[:, down]
        x_a, x_b, x_c = cos_in + sin_in, sin_in, cos_in
        g_a, g_b, g_c = cos_grad, cos_grad - sin_grad, cos_grad + sin_grad
        if half == 0:
            x_a = jnp.where(first, 0.0, x_a)
            x_b = jnp.where(first, -cos_in, x_b)
            x_c = jnp.where(first, -sin_in, x_c)
            g_b = jnp.where(first, cos_grad, g_b)
            g_c = jnp.where(first, sin_grad, g_c)
        for ref, value in ((xa, x_a), (xb, x_b), (xc, x_c), (ga, g_a), (gb, g_b), (gc, g_c)):
            ref[half] = value

    sign = jnp.where(lax.broadcasted_iota(jnp.int32, (8, LANES), 1) % 2 == 0, 1.0, -1.0)
    width = 4

    def one_half(half, carry):
        def at(ref, j):
            return ref[half, j * 8 : (j + 1) * 8, :]

        after = [jnp.zeros((8, LANES), F32)] * 2
        for k0 in reversed(range(0, NBLK, width)):
            sums = [[None] * width for _ in range(3)]
            for i in range(k0, NBLK):
                grads = [at(ref, i) for ref in (ga, gb, gc)]
                for kk in range(width):
                    j = i - k0 - kk
                    if j < 0:
                        continue
                    for n, ref in enumerate((xa, xb, xc)):
                        product = grads[n] * at(ref, j)
                        sums[n][kk] = product if sums[n][kk] is None else sums[n][kk] + product
            for kk in reversed(range(width)):
                k = k0 + kk
                now = [sums[0][kk] - sums[1][kk], sums[0][kk] - sums[2][kk]]
                for part in range(2):
                    total = now[part] + sign * after[part]
                    total = total + pltpu.roll(total, 4, 0)
                    for core in range(2):
                        zed[part * 2 + half, core * 64 + 2 * k : core * 64 + 2 * k + 2, :] = total[2 * core : 2 * core + 2]
                after = now
        return carry

    lax.fori_loop(0, 2, one_half, 0)
    z = jnp.concatenate([zed[n] for n in range(4)], axis=1)
    z_high = z.astype(BF16)
    z_low = (z - z_high.astype(F32)).astype(BF16)
    high = high_ref[...]
    y = dot(z_high, high) + (dot(z_low, high) + dot(z_high, low_ref[...]))
    for lh in range(2):
        ybuf[pl.ds(lh, LANES, stride=2), :] = y[:, lh * LANES : (lh + 1) * LANES]
    y = ybuf[...].astype(BF16)
    for x in range(4):
        out_ref[x * BLK : (x + 1) * BLK, :] = y


def total_kernel(parts_ref, out_ref):
    total = parts_ref[0:LANES].astype(F32)
    for n in range(1, 8):
        total = total + parts_ref[n * LANES : (n + 1) * LANES].astype(F32)
    row = lax.broadcasted_iota(jnp.int32, (512, LANES), 0)
    col = lax.broadcasted_iota(jnp.int32, (512, LANES), 1)
    repeat = jnp.where(col == (row >> 4) * 4 + (row & 3), 1.0, 0.0).astype(BF16)
    out_ref[...] = dot(repeat, total.astype(BF16)).astype(BF16)


def unpack_kernel(rows_ref, out_hbm, held, sems):
    def source(m):
        lh, core, c, p = m >> 7, (m >> 6) & 1, (m >> 5) & 1, m & 31
        return (p * 2 + core) * 4 + c * 2 + lh

    perm = permutation(source)
    halves = [dot(perm, rows_ref[part * BLK : (part + 1) * BLK, :]) for part in range(2)]
    copies = []
    for lh in range(2):
        rows = slice(lh * LANES, (lh + 1) * LANES)
        for core in range(2):
            at = lh * 128 + core * 64
            block = jnp.concatenate([halves[part][at + c * 32 : at + c * 32 + 32] for c in range(2) for part in range(2)], axis=0)
            held[rows, core * LANES : (core + 1) * LANES] = jnp.transpose(block)
        copies.append(pltpu.make_async_copy(held.at[rows], out_hbm.at[rows], sems.at[lh]))
        copies[-1].start()
    for copy in copies:
        copy.wait()


def call(kernel, shape, dtype, ins, out, scratch=()):
    return pl.pallas_call(
        kernel,
        out_shape=jax.ShapeDtypeStruct(shape, dtype),
        in_specs=[pl.BlockSpec(memory_space=space) for space in ins],
        out_specs=pl.BlockSpec(memory_space=out),
        scratch_shapes=list(scratch),
        compiler_params=pltpu.CompilerParams(vmem_limit_bytes=LIMIT),
    )


VMEM, HBM = pltpu.VMEM, pltpu.HBM
TWO_SEMS = pltpu.SemaphoreType.DMA((2,))
PACK = call(pack_kernel, (1024, LANES), BF16, [HBM] * 2, VMEM, [VMEM((2, BLK, BLK), BF16), TWO_SEMS])
CORRELATE = call(
    correlate_kernel,
    (1024, LANES),
    BF16,
    [VMEM] * 4,
    VMEM,
    [VMEM((2, BLK, LANES), F32)] * 6 + [VMEM((4, LANES, LANES), F32), VMEM((BLK, LANES), F32)],
)
TOTAL = call(total_kernel, (512, LANES), BF16, [VMEM], VMEM)
UNPACK = call(unpack_kernel, (BLK, BLK), F32, [VMEM], HBM, [VMEM((BLK, BLK), F32), TWO_SEMS])


def on_device(inputs, out_grads):
    rows = PACK(*[pltpu.with_memory_space_constraint(a[0], HBM) for a in (inputs, out_grads)])
    rows = exchange(rows, HALF_GROUPS)
    parts = CORRELATE(rows, *make_tables())
    parts = exchange(parts, SUM_GROUPS)
    rows = TOTAL(parts)
    rows = exchange(rows, PLANE_GROUPS)
    return UNPACK(rows)


def solution(mesh):
    in_specs = (P("dp", "ctx", None), P("dp", "ctx", None))
    out_specs = P("ctx", None)
    return jax.shard_map(on_device, mesh=mesh, in_specs=in_specs, out_specs=out_specs, check_vma=False)
```

time: 67.3 us -> 66.9 us (level)
  local copies, waits for them, and re-layouts: 1.82 us -> 0.02 us
  Pallas kernels: 3.78 us -> 4.65 us
    unnamed x10 -> x6, local copies, waits for them, and re-layouts: 1.82 us -> 0.02 us
    pallas_call x4, Pallas kernels: 3.78 us -> 4.65 us  [the longest x1 2.01 us: on_device(): parts = CORRELATE(rows, *make_tables())]
where the time goes in v2:
time: 66.9 us; the launch traced here: 66.6 us
  blocking collectives  61.9 us (93%)
  Pallas kernels  4.65 us (7%)
    all_to_all x3, blocking collectives, exchange(): lax.all_to_all(rows, ('dp', 'ctx'), 0, 0, axis_index_groups=groups, tiled...  61.9 us
    pallas_call x1, Pallas kernels, on_device(): parts = CORRELATE(rows, *make_tables())  2.01 us
    pallas_call x1, Pallas kernels, on_device(): PACK(*[pltpu.with_memory_space_constraint(a[0], HBM) for a in (inputs, ou...  1.44 us

profile of v2, /device:TPU:1, one launch (start us, length us, event | category | flops | bytes accessed | tf_op | source)
XLA Modules:
  0.0 66.6 jit_solution(16881917646397382490)
XLA Ops:
  0.0 0.0 copy-start.2
  0.0 1.4 %shard_map.55 = bf16[1024,128]{1,0:T(8,128)(2,1)S(1)} custom-call(bf16[256,256]{1,0:T(8,128)(2,1)} %bitcast.14, bf16[256,256]{1,0:T(8,128)(2,1)} %bitcast.15), custom_call_target="tpu_custom_call" | custom-call | tf_op jit(solution)/shard_map/pallas_call | solution.py:223
  1.5 0.0 copy-start
  1.5 0.0 copy-start.1
  1.5 29.7 %all_to_all.33 = bf16[64,16,128]{2,1,0:T(8,128)(2,1)S(1)} all-to-all(bf16[64,16,128]{2,1,0:T(8,128)(2,1)S(1)} %bitcast.11), channel_id=1, replica_groups={{0,64,1,65,2,66,3,67,4,68,5,69,6,70,7,71,8,72,9,73,10,74,11,75,12,76,13..., dimensions={0} | all-to-all | bytes 524288 | tf_op jit(solution)/shard_map/all_to_all | solution.py:43
  31.2 0.0 copy-done.2
  31.2 0.0 copy-done
  31.2 0.0 copy-done.1
  31.2 2.0 %shard_map.56 = bf16[1024,128]{1,0:T(8,128)(2,1)S(1)} custom-call(bf16[1024,128]{1,0:T(8,128)(2,1)S(1)} %bitcast.8, bf16[256,512]{1,0:T(8,128)(2,1)S(1)} %copy-done.2, bf16[512,256]{1,0:T(8,128)(2,1)S(1)} %copy-done.1, bf16[512,256]{1,0:T(8,128)(2,1)S(1)} %copy-done), custom_call_target="tpu_custom_call" | custom-call | tf_op jit(solution)/shard_map/pallas_call | solution.py:225
  33.2 13.8 %all_to_all.34 = bf16[8,128,128]{2,1,0:T(8,128)(2,1)S(1)} all-to-all(bf16[8,128,128]{2,1,0:T(8,128)(2,1)S(1)} %bitcast.9), channel_id=1, replica_groups={{0,32,128,160,256,288,384,416},{1,33,129,161,257,289,385,417},{2,34,130..., dimensions={0} | all-to-all | bytes 524288 | tf_op jit(solution)/shard_map/all_to_all | solution.py:43
  47.0 0.2 shard_map.57
  47.3 18.4 %all_to_all.35 = bf16[128,4,128]{2,1,0:T(4,128)(2,1)S(1)} all-to-all(bf16[128,4,128]{2,1,0:T(4,128)(2,1)S(1)} %bitcast.12), channel_id=1, replica_groups={{0,32,64,96,1,33,65,97,2,34,66,98,3,35,67,99,4,36,68,100,5,37,69,101,6,..., dimensions={0} | all-to-all | bytes 262144 | tf_op jit(solution)/shard_map/all_to_all | solution.py:43
  65.7 1.0 %shard_map.58 = f32[256,256]{1,0:T(8,128)} custom-call(bf16[512,128]{1,0:T(8,128)(2,1)S(1)} %bitcast.13), custom_call_target="tpu_custom_call" | custom-call | tf_op jit(solution)/shard_map/pallas_call | solution.py:229
Async XLA Ops:
  0.0 31.2 %copy-start.2 = (bf16[256,512]{1,0:T(8,128)(2,1)S(1)}, bf16[256,512]{1,0:T(8,128)(2,1)}, u32[]{:S(2)}) copy-start(bf16[256,512]{1,0:T(8,128)(2,1)} %constant.6.clone.forward_ref) | copy-start | bytes 786436
  1.5 29.8 %copy-start = (bf16[512,256]{1,0:T(8,128)(2,1)S(1)}, bf16[512,256]{1,0:T(8,128)(2,1)}, u32[]{:S(2)}) copy-start(bf16[512,256]{1,0:T(8,128)(2,1)} %constant.8.clone.low_ref) | copy-start | bytes 786436
  1.5 29.7 %copy-start.1 = (bf16[512,256]{1,0:T(8,128)(2,1)S(1)}, bf16[512,256]{1,0:T(8,128)(2,1)}, u32[]{:S(2)}) copy-start(bf16[512,256]{1,0:T(8,128)(2,1)} %constant.7.clone.high_ref) | copy-start | bytes 786436

commit v3 on v2

--- a/solution.py
+++ b/solution.py
@@ -19,12 +19,19 @@
 LIMIT = 48 * 1024 * 1024
 
 
+FIRST = {"x": 2, "y_lo": 0, "core": 0, "z": 6, "y_hi": 2}
+
+
+def turned_range(axis):
+    return [(n + FIRST[axis]) % SIZES[axis] for n in range(SIZES[axis])]
+
+
 def groups_over(axes):
     rest = [a for a in SIZES if a not in axes]
     groups = []
     for fixed in itertools.product(*[range(SIZES[a]) for a in rest]):
         group = []
-        for moving in itertools.product(*[range(SIZES[a]) for a in axes]):
+        for moving in itertools.product(*[turned_range(a) for a in axes]):
             place = dict(zip(rest, fixed)) | dict(zip(axes, moving))
             flat = 0
             for a in SIZES:
@@ -33,6 +40,10 @@
         groups.append(group)
     return groups
 
+
+SLOT = [0] * NBLK
+for place, (z, y) in enumerate(itertools.product(turned_range("z"), turned_range("y_hi"))):
+    SLOT[z * SIZES["y_hi"] + y] = place
 
 HALF_GROUPS = groups_over(("z", "y_hi", "y_lo"))
 SUM_GROUPS = groups_over(("x", "core"))
@@ -123,9 +134,9 @@
     sign = jnp.where(lax.broadcasted_iota(jnp.int32, (8, LANES), 1) % 2 == 0, 1.0, -1.0)
     width = 4
 
-    def one_half(half, carry):
+    for half in range(2):
         def at(ref, j):
-            return ref[half, j * 8 : (j + 1) * 8, :]
+            return ref[half, SLOT[j] * 8 : (SLOT[j] + 1) * 8, :]
 
         after = [jnp.zeros((8, LANES), F32)] * 2
         for k0 in reversed(range(0, NBLK, width)):
@@ -146,11 +157,9 @@
                     total = now[part] + sign * after[part]
                     total = total + pltpu.roll(total, 4, 0)
                     for core in range(2):
-                        zed[part * 2 + half, core * 64 + 2 * k : core * 64 + 2 * k + 2, :] = total[2 * core : 2 * core + 2]
+                        at_row = core * 64 + 2 * SLOT[k]
+                        zed[part * 2 + half, at_row : at_row + 2, :] = total[2 * core : 2 * core + 2]
                 after = now
-        return carry
-
-    lax.fori_loop(0, 2, one_half, 0)
     z = jnp.concatenate([zed[n] for n in range(4)], axis=1)
     z_high = z.astype(BF16)
     z_low = (z - z_high.astype(F32)).astype(BF16)

time: 66.9 us -> 59.6 us (0.89)
  blocking collectives: 61.9 us -> 54.8 us
    all_to_all x3, blocking collectives: 61.9 us -> 54.8 us  [exchange(): lax.all_to_all(rows, ('dp', 'ctx'), 0, 0, axis_index_groups=groups, tiled...]
where the time goes in v3:
time: 59.6 us; the launch traced here: 59.3 us
  blocking collectives  54.8 us (92%)
  Pallas kernels  4.48 us (8%)
    all_to_all x3, blocking collectives, exchange(): lax.all_to_all(rows, ('dp', 'ctx'), 0, 0, axis_index_groups=groups, tiled...  54.8 us
    pallas_call x1, Pallas kernels, on_device(): parts = CORRELATE(rows, *make_tables())  1.84 us
    pallas_call x1, Pallas kernels, on_device(): PACK(*[pltpu.with_memory_space_constraint(a[0], HBM) for a in (inputs, ou...  1.44 us

profile of v3, /device:TPU:1, one launch (start us, length us, event | category | flops | bytes accessed | tf_op | source)
XLA Modules:
  0.0 59.3 jit_solution(5218542960436422088)
XLA Ops:
  0.0 0.0 copy-start.2
  0.0 1.4 %shard_map.55 = bf16[1024,128]{1,0:T(8,128)(2,1)S(1)} custom-call(bf16[256,256]{1,0:T(8,128)(2,1)} %bitcast.14, bf16[256,256]{1,0:T(8,128)(2,1)} %bitcast.15), custom_call_target="tpu_custom_call" | custom-call | tf_op jit(solution)/shard_map/pallas_call | solution.py:232
  1.5 0.0 copy-start
  1.5 0.0 copy-start.1
  1.5 26.0 %all_to_all.33 = bf16[64,16,128]{2,1,0:T(8,128)(2,1)S(1)} all-to-all(bf16[64,16,128]{2,1,0:T(8,128)(2,1)S(1)} %bitcast.11), channel_id=1, replica_groups={{26,90,27,91,24,88,25,89,30,94,31,95,28,92,29,93,2,66,3,67,0,64,1,65,6,..., dimensions={0} | all-to-all | bytes 524288 | tf_op jit(solution)/shard_map/all_to_all | solution.py:54
  27.5 0.0 copy-done.2
  27.5 0.0 copy-done
  27.5 0.0 copy-done.1
  27.5 1.8 %shard_map.56 = bf16[1024,128]{1,0:T(8,128)(2,1)S(1)} custom-call(bf16[1024,128]{1,0:T(8,128)(2,1)S(1)} %bitcast.8, bf16[256,512]{1,0:T(8,128)(2,1)S(1)} %copy-done.2, bf16[512,256]{1,0:T(8,128)(2,1)S(1)} %copy-done.1, bf16[512,256]{1,0:T(8,128)(2,1)S(1)} %copy-done), custom_call_target="tpu_custom_call" | custom-call | tf_op jit(solution)/shard_map/pallas_call | solution.py:234
  29.3 10.9 %all_to_all.34 = bf16[8,128,128]{2,1,0:T(8,128)(2,1)S(1)} all-to-all(bf16[8,128,128]{2,1,0:T(8,128)(2,1)S(1)} %bitcast.9), channel_id=1, replica_groups={{256,288,384,416,0,32,128,160},{257,289,385,417,1,33,129,161},{258,290,..., dimensions={0} | all-to-all | bytes 524288 | tf_op jit(solution)/shard_map/all_to_all | solution.py:54
  40.3 0.2 shard_map.57
  40.5 17.9 %all_to_all.35 = bf16[128,4,128]{2,1,0:T(4,128)(2,1)S(1)} all-to-all(bf16[128,4,128]{2,1,0:T(4,128)(2,1)S(1)} %bitcast.12), channel_id=1, replica_groups={{26,58,90,122,27,59,91,123,24,56,88,120,25,57,89,121,30,62,94,126,31,63..., dimensions={0} | all-to-all | bytes 262144 | tf_op jit(solution)/shard_map/all_to_all | solution.py:54
  58.4 1.0 %shard_map.58 = f32[256,256]{1,0:T(8,128)} custom-call(bf16[512,128]{1,0:T(8,128)(2,1)S(1)} %bitcast.13), custom_call_target="tpu_custom_call" | custom-call | tf_op jit(solution)/shard_map/pallas_call | solution.py:238
Async XLA Ops:
  0.0 27.5 %copy-start.2 = (bf16[256,512]{1,0:T(8,128)(2,1)S(1)}, bf16[256,512]{1,0:T(8,128)(2,1)}, u32[]{:S(2)}) copy-start(bf16[256,512]{1,0:T(8,128)(2,1)} %constant.6.clone.forward_ref) | copy-start | bytes 786436
  1.5 26.0 %copy-start = (bf16[512,256]{1,0:T(8,128)(2,1)S(1)}, bf16[512,256]{1,0:T(8,128)(2,1)}, u32[]{:S(2)}) copy-start(bf16[512,256]{1,0:T(8,128)(2,1)} %constant.8.clone.low_ref) | copy-start | bytes 786436
  1.5 26.0 %copy-start.1 = (bf16[512,256]{1,0:T(8,128)(2,1)S(1)}, bf16[512,256]{1,0:T(8,128)(2,1)}, u32[]{:S(2)}) copy-start(bf16[512,256]{1,0:T(8,128)(2,1)} %constant.7.clone.high_ref) | copy-start | bytes 786436

commit v4 on v3

--- a/solution.py
+++ b/solution.py
@@ -19,7 +19,7 @@
 LIMIT = 48 * 1024 * 1024
 
 
-FIRST = {"x": 2, "y_lo": 0, "core": 0, "z": 6, "y_hi": 2}
+FIRST = {"x": 2, "y_lo": 0, "core": 0, "z": 5, "y_hi": 2}
 
 
 def turned_range(axis):
@@ -45,9 +45,8 @@
 for place, (z, y) in enumerate(itertools.product(turned_range("z"), turned_range("y_hi"))):
     SLOT[z * SIZES["y_hi"] + y] = place
 
-HALF_GROUPS = groups_over(("z", "y_hi", "y_lo"))
-SUM_GROUPS = groups_over(("x", "core"))
 PLANE_GROUPS = groups_over(("z", "y_hi", "y_lo", "core"))
+X_GROUPS = groups_over(("x",))
 
 
 def exchange(rows, groups):
@@ -64,10 +63,7 @@
     forward = np.concatenate([np.cos(angle), sines], axis=0)
     weight = np.where(freq == 0, 1.0, 2.0) / span
     back = np.concatenate([weight * np.cos(angle), np.where(freq == 0, signs / span, -weight * np.sin(angle))], axis=0)
-    back = back.astype(np.float32)
-    high = back.astype(ml_dtypes.bfloat16)
-    low = (back - high.astype(np.float32)).astype(ml_dtypes.bfloat16)
-    return forward.T.astype(ml_dtypes.bfloat16), high, low
+    return forward.T.astype(ml_dtypes.bfloat16), back.astype(ml_dtypes.bfloat16)
 
 
 def dot(a, b):
@@ -84,25 +80,25 @@
     copies = [pltpu.make_async_copy(ref, held.at[a], sems.at[a]) for a, ref in enumerate((in_hbm, grad_hbm))]
     for copy in copies:
         copy.start()
-    perm = permutation(lambda m: (m & 15) * 16 + (m >> 4))
+    perm = permutation(lambda m: (m & 7) * 32 + (m >> 3))
     turned = []
     for a in range(2):
         copies[a].wait()
-        turned.append(jnp.transpose(held[a].astype(F32)).astype(BF16))
+        turned.append(jnp.transpose(held[a]))
     for part in range(4):
         pieces = []
         for a in range(2):
-            for c in range(4):
+            for c in range(2):
                 for th in range(2):
-                    start = c * 64 + part * 16
-                    pieces.append(turned[a][start : start + 16, th * LANES : (th + 1) * LANES])
+                    start = c * LANES + part * 32
+                    pieces.append(turned[a][start : start + 32, th * LANES : (th + 1) * LANES])
         out_ref[part * BLK : (part + 1) * BLK, :] = dot(perm, jnp.concatenate(pieces, axis=0)).astype(BF16)
 
 
-def correlate_kernel(rows_ref, forward_ref, high_ref, low_ref, out_ref, xa, xb, xc, ga, gb, gc, zed, ybuf):
+def correlate_kernel(rows_ref, forward_ref, back_ref, out_ref, xa, xb, xc, ga, gb, gc, zed, ybuf):
     def source(m):
-        a, th, j8, r, c = m >> 7, (m >> 6) & 1, (m >> 3) & 7, (m >> 2) & 1, m & 3
-        return j8 * 32 + r * 16 + a * 8 + c * 2 + th
+        a, th, j8, r, c = m >> 7, (m >> 6) & 1, (m >> 3) & 7, (m >> 1) & 3, m & 1
+        return j8 * 32 + r * 8 + a * 4 + c * 2 + th
 
     perm = permutation(source)
     blocks = [[], []]
@@ -156,25 +152,21 @@
                 for part in range(2):
                     total = now[part] + sign * after[part]
                     total = total + pltpu.roll(total, 4, 0)
-                    for core in range(2):
-                        at_row = core * 64 + 2 * SLOT[k]
-                        zed[part * 2 + half, at_row : at_row + 2, :] = total[2 * core : 2 * core + 2]
+                    total = total + pltpu.roll(total, 2, 0)
+                    zed[part * 2 + half, 2 * SLOT[k] : 2 * SLOT[k] + 2, :] = total[0:2]
                 after = now
     z = jnp.concatenate([zed[n] for n in range(4)], axis=1)
-    z_high = z.astype(BF16)
-    z_low = (z - z_high.astype(F32)).astype(BF16)
-    high = high_ref[...]
-    y = dot(z_high, high) + (dot(z_low, high) + dot(z_high, low_ref[...]))
+    y = dot(z.astype(BF16), back_ref[...])
     for lh in range(2):
-        ybuf[pl.ds(lh, LANES, stride=2), :] = y[:, lh * LANES : (lh + 1) * LANES]
+        ybuf[pl.ds(lh, 64, stride=2), :] = y[:, lh * LANES : (lh + 1) * LANES]
     y = ybuf[...].astype(BF16)
     for x in range(4):
-        out_ref[x * BLK : (x + 1) * BLK, :] = y
+        out_ref[x * LANES : (x + 1) * LANES, :] = y
 
 
 def total_kernel(parts_ref, out_ref):
     total = parts_ref[0:LANES].astype(F32)
-    for n in range(1, 8):
+    for n in range(1, 4):
         total = total + parts_ref[n * LANES : (n + 1) * LANES].astype(F32)
     row = lax.broadcasted_iota(jnp.int32, (512, LANES), 0)
     col = lax.broadcasted_iota(jnp.int32, (512, LANES), 1)
@@ -183,19 +175,15 @@
 
 
 def unpack_kernel(rows_ref, out_hbm, held, sems):
-    def source(m):
-        lh, core, c, p = m >> 7, (m >> 6) & 1, (m >> 5) & 1, m & 31
-        return (p * 2 + core) * 4 + c * 2 + lh
-
-    perm = permutation(source)
+    perm = permutation(lambda m: (m & 63) * 4 + (m >> 6))
     halves = [dot(perm, rows_ref[part * BLK : (part + 1) * BLK, :]) for part in range(2)]
     copies = []
     for lh in range(2):
         rows = slice(lh * LANES, (lh + 1) * LANES)
-        for core in range(2):
-            at = lh * 128 + core * 64
-            block = jnp.concatenate([halves[part][at + c * 32 : at + c * 32 + 32] for c in range(2) for part in range(2)], axis=0)
-            held[rows, core * LANES : (core + 1) * LANES] = jnp.transpose(block)
+        for c in range(2):
+            at = (c * 2 + lh) * 64
+            block = jnp.concatenate([halves[part][at : at + 64] for part in range(2)], axis=0)
+            held[rows, c * LANES : (c + 1) * LANES] = jnp.transpose(block)
         copies.append(pltpu.make_async_copy(held.at[rows], out_hbm.at[rows], sems.at[lh]))
         copies[-1].start()
     for copy in copies:
@@ -218,11 +206,11 @@
 PACK = call(pack_kernel, (1024, LANES), BF16, [HBM] * 2, VMEM, [VMEM((2, BLK, BLK), BF16), TWO_SEMS])
 CORRELATE = call(
     correlate_kernel,
-    (1024, LANES),
+    (512, LANES),
     BF16,
-    [VMEM] * 4,
+    [VMEM] * 3,
     VMEM,
-    [VMEM((2, BLK, LANES), F32)] * 6 + [VMEM((4, LANES, LANES), F32), VMEM((BLK, LANES), F32)],
+    [VMEM((2, BLK, LANES), F32)] * 6 + [VMEM((4, 64, LANES), F32), VMEM((LANES, LANES), F32)],
 )
 TOTAL = call(total_kernel, (512, LANES), BF16, [VMEM], VMEM)
 UNPACK = call(unpack_kernel, (BLK, BLK), F32, [VMEM], HBM, [VMEM((BLK, BLK), F32), TWO_SEMS])
@@ -230,9 +218,9 @@
 
 def on_device(inputs, out_grads):
     rows = PACK(*[pltpu.with_memory_space_constraint(a[0], HBM) for a in (inputs, out_grads)])
-    rows = exchange(rows, HALF_GROUPS)
+    rows = exchange(rows, PLANE_GROUPS)
     parts = CORRELATE(rows, *make_tables())
-    parts = exchange(parts, SUM_GROUPS)
+    parts = exchange(parts, X_GROUPS)
     rows = TOTAL(parts)
     rows = exchange(rows, PLANE_GROUPS)
     return UNPACK(rows)

time: 59.6 us -> 58.7 us (0.985)
  no operation moved by 1% of the time
where the time goes in v4:
time: 58.7 us; the launch traced here: 58.5 us
  blocking collectives  54.3 us (93%)
  Pallas kernels  4.12 us (7%)
    all_to_all x3, blocking collectives, exchange(): lax.all_to_all(rows, ('dp', 'ctx'), 0, 0, axis_index_groups=groups, tiled...  54.3 us
    pallas_call x1, Pallas kernels, on_device(): parts = CORRELATE(rows, *make_tables())  1.57 us
    pallas_call x1, Pallas kernels, on_device(): PACK(*[pltpu.with_memory_space_constraint(a[0], HBM) for a in (inputs, ou...  1.36 us

profile of v4, /device:TPU:1, one launch (start us, length us, event | category | flops | bytes accessed | tf_op | source)
XLA Modules:
  0.0 58.5 jit_solution(11053574373269528798)
XLA Ops:
  0.0 1.4 %shard_map.46 = bf16[1024,128]{1,0:T(8,128)(2,1)S(1)} custom-call(bf16[256,256]{1,0:T(8,128)(2,1)} %bitcast.14, bf16[256,256]{1,0:T(8,128)(2,1)} %bitcast.15), custom_call_target="tpu_custom_call" | custom-call | tf_op jit(solution)/shard_map/pallas_call | solution.py:220
  1.4 0.0 copy-start
  1.4 0.0 copy-start.1
  1.4 28.5 %all_to_all.33 = bf16[128,8,128]{2,1,0:T(8,128)(2,1)S(1)} all-to-all(bf16[128,8,128]{2,1,0:T(8,128)(2,1)S(1)} %bitcast.9), channel_id=1, replica_groups={{22,54,86,118,23,55,87,119,20,52,84,116,21,53,85,117,26,58,90,122,27,59..., dimensions={0} | all-to-all | bytes 524288 | tf_op jit(solution)/shard_map/all_to_all | solution.py:53
  29.8 0.0 copy-done
  29.8 0.0 copy-done.1
  29.8 1.6 %shard_map.47 = bf16[512,128]{1,0:T(8,128)(2,1)S(1)} custom-call(bf16[1024,128]{1,0:T(8,128)(2,1)S(1)} %bitcast.8, bf16[256,512]{1,0:T(8,128)(2,1)S(1)} %copy-done.1, bf16[512,256]{1,0:T(8,128)(2,1)S(1)} %copy-done), custom_call_target="tpu_custom_call" | custom-call | tf_op jit(solution)/shard_map/pallas_call | solution.py:222
  31.4 7.6 %all_to_all.34 = bf16[4,128,128]{2,1,0:T(8,128)(2,1)S(1)} all-to-all(bf16[4,128,128]{2,1,0:T(8,128)(2,1)S(1)} %bitcast.10), channel_id=1, replica_groups={{256,384,0,128},{257,385,1,129},{258,386,2,130},{259,387,3,131},{260,38..., dimensions={0} | all-to-all | bytes 262144 | tf_op jit(solution)/shard_map/all_to_all | solution.py:53
  39.0 0.2 shard_map.48
  39.2 18.3 %all_to_all.35 = bf16[128,4,128]{2,1,0:T(4,128)(2,1)S(1)} all-to-all(bf16[128,4,128]{2,1,0:T(4,128)(2,1)S(1)} %bitcast.13), channel_id=1, replica_groups={{22,54,86,118,23,55,87,119,20,52,84,116,21,53,85,117,26,58,90,122,27,59..., dimensions={0} | all-to-all | bytes 262144 | tf_op jit(solution)/shard_map/all_to_all | solution.py:53
  57.5 1.0 %shard_map.49 = f32[256,256]{1,0:T(8,128)} custom-call(bf16[512,128]{1,0:T(8,128)(2,1)S(1)} %bitcast.11), custom_call_target="tpu_custom_call" | custom-call | tf_op jit(solution)/shard_map/pallas_call | solution.py:226
Async XLA Ops:
  1.4 28.5 %copy-start = (bf16[512,256]{1,0:T(8,128)(2,1)S(1)}, bf16[512,256]{1,0:T(8,128)(2,1)}, u32[]{:S(2)}) copy-start(bf16[512,256]{1,0:T(8,128)(2,1)} %constant.5.clone.back_ref) | copy-start | bytes 786436
  1.4 28.5 %copy-start.1 = (bf16[256,512]{1,0:T(8,128)(2,1)S(1)}, bf16[256,512]{1,0:T(8,128)(2,1)}, u32[]{:S(2)}) copy-start(bf16[256,512]{1,0:T(8,128)(2,1)} %constant.4.clone.forward_ref) | copy-start | bytes 786436

commit v5 on v4

--- a/solution.py
+++ b/solution.py
@@ -19,7 +19,7 @@
 LIMIT = 48 * 1024 * 1024
 
 
-FIRST = {"x": 2, "y_lo": 0, "core": 0, "z": 5, "y_hi": 2}
+FIRST = {"x": 2, "y_lo": 0, "core": 1, "z": 5, "y_hi": 2}
 
 
 def turned_range(axis):

time: 58.7 us -> 57.8 us (0.985)
  blocking collectives: 54.3 us -> 53.4 us
    all_to_all x3, blocking collectives: 54.3 us -> 53.4 us  [exchange(): lax.all_to_all(rows, ('dp', 'ctx'), 0, 0, axis_index_groups=groups, tiled...]
where the time goes in v5:
time: 57.8 us; the launch traced here: 57.6 us
  blocking collectives  53.4 us (92%)
  Pallas kernels  4.13 us (7%)
    all_to_all x3, blocking collectives, exchange(): lax.all_to_all(rows, ('dp', 'ctx'), 0, 0, axis_index_groups=groups, tiled...  53.4 us
    pallas_call x1, Pallas kernels, on_device(): parts = CORRELATE(rows, *make_tables())  1.57 us
    pallas_call x1, Pallas kernels, on_device(): PACK(*[pltpu.with_memory_space_constraint(a[0], HBM) for a in (inputs, ou...  1.36 us

profile of v5, /device:TPU:1, one launch (start us, length us, event | category | flops | bytes accessed | tf_op | source)
XLA Modules:
  0.0 57.6 jit_solution(9400109577669799332)
XLA Ops:
  0.0 1.4 %shard_map.46 = bf16[1024,128]{1,0:T(8,128)(2,1)S(1)} custom-call(bf16[256,256]{1,0:T(8,128)(2,1)} %bitcast.14, bf16[256,256]{1,0:T(8,128)(2,1)} %bitcast.15), custom_call_target="tpu_custom_call" | custom-call | tf_op jit(solution)/shard_map/pallas_call | solution.py:220
  1.4 0.0 copy-start
  1.4 0.0 copy-start.1
  1.4 28.1 %all_to_all.33 = bf16[128,8,128]{2,1,0:T(8,128)(2,1)S(1)} all-to-all(bf16[128,8,128]{2,1,0:T(8,128)(2,1)S(1)} %bitcast.9), channel_id=1, replica_groups={{54,22,118,86,55,23,119,87,52,20,116,84,53,21,117,85,58,26,122,90,59,27..., dimensions={0} | all-to-all | bytes 524288 | tf_op jit(solution)/shard_map/all_to_all | solution.py:53
  29.5 0.0 copy-done
  29.5 0.0 copy-done.1
  29.5 1.6 %shard_map.47 = bf16[512,128]{1,0:T(8,128)(2,1)S(1)} custom-call(bf16[1024,128]{1,0:T(8,128)(2,1)S(1)} %bitcast.8, bf16[256,512]{1,0:T(8,128)(2,1)S(1)} %copy-done.1, bf16[512,256]{1,0:T(8,128)(2,1)S(1)} %copy-done), custom_call_target="tpu_custom_call" | custom-call | tf_op jit(solution)/shard_map/pallas_call | solution.py:222
  31.1 7.6 %all_to_all.34 = bf16[4,128,128]{2,1,0:T(8,128)(2,1)S(1)} all-to-all(bf16[4,128,128]{2,1,0:T(8,128)(2,1)S(1)} %bitcast.10), channel_id=1, replica_groups={{256,384,0,128},{257,385,1,129},{258,386,2,130},{259,387,3,131},{260,38..., dimensions={0} | all-to-all | bytes 262144 | tf_op jit(solution)/shard_map/all_to_all | solution.py:53
  38.7 0.2 shard_map.48
  38.9 17.7 %all_to_all.35 = bf16[128,4,128]{2,1,0:T(4,128)(2,1)S(1)} all-to-all(bf16[128,4,128]{2,1,0:T(4,128)(2,1)S(1)} %bitcast.13), channel_id=1, replica_groups={{54,22,118,86,55,23,119,87,52,20,116,84,53,21,117,85,58,26,122,90,59,27..., dimensions={0} | all-to-all | bytes 262144 | tf_op jit(solution)/shard_map/all_to_all | solution.py:53
  56.6 1.0 %shard_map.49 = f32[256,256]{1,0:T(8,128)} custom-call(bf16[512,128]{1,0:T(8,128)(2,1)S(1)} %bitcast.11), custom_call_target="tpu_custom_call" | custom-call | tf_op jit(solution)/shard_map/pallas_call | solution.py:226
Async XLA Ops:
  1.4 28.2 %copy-start = (bf16[512,256]{1,0:T(8,128)(2,1)S(1)}, bf16[512,256]{1,0:T(8,128)(2,1)}, u32[]{:S(2)}) copy-start(bf16[512,256]{1,0:T(8,128)(2,1)} %constant.5.clone.back_ref) | copy-start | bytes 786436
  1.4 28.1 %copy-start.1 = (bf16[256,512]{1,0:T(8,128)(2,1)S(1)}, bf16[256,512]{1,0:T(8,128)(2,1)}, u32[]{:S(2)}) copy-start(bf16[256,512]{1,0:T(8,128)(2,1)} %constant.4.clone.forward_ref) | copy-start | bytes 786436

commit v6 on v5

--- a/solution.py
+++ b/solution.py
@@ -45,7 +45,7 @@
 for place, (z, y) in enumerate(itertools.product(turned_range("z"), turned_range("y_hi"))):
     SLOT[z * SIZES["y_hi"] + y] = place
 
-PLANE_GROUPS = groups_over(("z", "y_hi", "y_lo", "core"))
+PLANE_GROUPS = groups_over(("core", "z", "y_hi", "y_lo"))
 X_GROUPS = groups_over(("x",))
 
 
@@ -97,13 +97,14 @@
 
 def correlate_kernel(rows_ref, forward_ref, back_ref, out_ref, xa, xb, xc, ga, gb, gc, zed, ybuf):
     def source(m):
-        a, th, j8, r, c = m >> 7, (m >> 6) & 1, (m >> 3) & 7, (m >> 1) & 3, m & 1
-        return j8 * 32 + r * 8 + a * 4 + c * 2 + th
+        a, th, j8, core, y, c = m >> 7, (m >> 6) & 1, (m >> 3) & 7, (m >> 2) & 1, (m >> 1) & 1, m & 1
+        return core * 128 + (j8 * 2 + y) * 8 + a * 4 + c * 2 + th
 
     perm = permutation(source)
     blocks = [[], []]
     for part in range(4):
-        q = dot(perm, rows_ref[part * BLK : (part + 1) * BLK, :]).astype(BF16)
+        both = [rows_ref[core * 512 + part * LANES : core * 512 + (part + 1) * LANES, :] for core in range(2)]
+        q = dot(perm, jnp.concatenate(both, axis=0)).astype(BF16)
         for a in range(2):
             at = a * 128
             blocks[a].append(jnp.concatenate([q[at : at + 64], q[at + 64 : at + 128]], axis=1))
@@ -170,7 +171,7 @@
         total = total + parts_ref[n * LANES : (n + 1) * LANES].astype(F32)
     row = lax.broadcasted_iota(jnp.int32, (512, LANES), 0)
     col = lax.broadcasted_iota(jnp.int32, (512, LANES), 1)
-    repeat = jnp.where(col == (row >> 4) * 4 + (row & 3), 1.0, 0.0).astype(BF16)
+    repeat = jnp.where(col == ((row >> 3) & 31) * 4 + (row & 3), 1.0, 0.0).astype(BF16)
     out_ref[...] = dot(repeat, total.astype(BF16)).astype(BF16)
 
 

time: 57.8 us -> 57.3 us (level)
  blocking collectives: 53.4 us -> 52.8 us
    all_to_all x3, blocking collectives: 53.4 us -> 52.8 us  [exchange(): lax.all_to_all(rows, ('dp', 'ctx'), 0, 0, axis_index_groups=groups, tiled...]
where the time goes in v6:
time: 57.3 us; the launch traced here: 57 us
  blocking collectives  52.8 us (92%)
  Pallas kernels  4.15 us (7%)
    all_to_all x3, blocking collectives, exchange(): lax.all_to_all(rows, ('dp', 'ctx'), 0, 0, axis_index_groups=groups, tiled...  52.8 us
    pallas_call x1, Pallas kernels, on_device(): parts = CORRELATE(rows, *make_tables())  1.59 us
    pallas_call x1, Pallas kernels, on_device(): PACK(*[pltpu.with_memory_space_constraint(a[0], HBM) for a in (inputs, ou...  1.36 us

profile of v6, /device:TPU:1, one launch (start us, length us, event | category | flops | bytes accessed | tf_op | source)
XLA Modules:
  0.0 57.0 jit_solution(10393524795939833452)
XLA Ops:
  0.0 1.4 %shard_map.46 = bf16[1024,128]{1,0:T(8,128)(2,1)S(1)} custom-call(bf16[256,256]{1,0:T(8,128)(2,1)} %bitcast.14, bf16[256,256]{1,0:T(8,128)(2,1)} %bitcast.15), custom_call_target="tpu_custom_call" | custom-call | tf_op jit(solution)/shard_map/pallas_call | solution.py:221
  1.4 0.0 copy-start
  1.4 0.0 copy-start.1
  1.4 27.7 %all_to_all.33 = bf16[128,8,128]{2,1,0:T(8,128)(2,1)S(1)} all-to-all(bf16[128,8,128]{2,1,0:T(8,128)(2,1)S(1)} %bitcast.9), channel_id=1, replica_groups={{54,118,55,119,52,116,53,117,58,122,59,123,56,120,57,121,62,126,63,127,..., dimensions={0} | all-to-all | bytes 524288 | tf_op jit(solution)/shard_map/all_to_all | solution.py:53
  29.1 0.0 copy-done
  29.1 0.0 copy-done.1
  29.1 1.6 %shard_map.47 = bf16[512,128]{1,0:T(8,128)(2,1)S(1)} custom-call(bf16[1024,128]{1,0:T(8,128)(2,1)S(1)} %bitcast.8, bf16[256,512]{1,0:T(8,128)(2,1)S(1)} %copy-done.1, bf16[512,256]{1,0:T(8,128)(2,1)S(1)} %copy-done), custom_call_target="tpu_custom_call" | custom-call | tf_op jit(solution)/shard_map/pallas_call | solution.py:223
  30.7 7.3 %all_to_all.34 = bf16[4,128,128]{2,1,0:T(8,128)(2,1)S(1)} all-to-all(bf16[4,128,128]{2,1,0:T(8,128)(2,1)S(1)} %bitcast.10), channel_id=1, replica_groups={{256,384,0,128},{257,385,1,129},{258,386,2,130},{259,387,3,131},{260,38..., dimensions={0} | all-to-all | bytes 262144 | tf_op jit(solution)/shard_map/all_to_all | solution.py:53
  38.0 0.2 shard_map.48
  38.2 17.8 %all_to_all.35 = bf16[128,4,128]{2,1,0:T(4,128)(2,1)S(1)} all-to-all(bf16[128,4,128]{2,1,0:T(4,128)(2,1)S(1)} %bitcast.13), channel_id=1, replica_groups={{54,118,55,119,52,116,53,117,58,122,59,123,56,120,57,121,62,126,63,127,..., dimensions={0} | all-to-all | bytes 262144 | tf_op jit(solution)/shard_map/all_to_all | solution.py:53
  56.0 1.0 %shard_map.49 = f32[256,256]{1,0:T(8,128)} custom-call(bf16[512,128]{1,0:T(8,128)(2,1)S(1)} %bitcast.11), custom_call_target="tpu_custom_call" | custom-call | tf_op jit(solution)/shard_map/pallas_call | solution.py:227
Async XLA Ops:
  1.4 27.7 %copy-start = (bf16[512,256]{1,0:T(8,128)(2,1)S(1)}, bf16[512,256]{1,0:T(8,128)(2,1)}, u32[]{:S(2)}) copy-start(bf16[512,256]{1,0:T(8,128)(2,1)} %constant.5.clone.back_ref) | copy-start | bytes 786436
  1.4 27.7 %copy-start.1 = (bf16[256,512]{1,0:T(8,128)(2,1)S(1)}, bf16[256,512]{1,0:T(8,128)(2,1)}, u32[]{:S(2)}) copy-start(bf16[256,512]{1,0:T(8,128)(2,1)} %constant.4.clone.forward_ref) | copy-start | bytes 786436

commit v7 on v6

--- a/solution.py
+++ b/solution.py
@@ -19,11 +19,13 @@
 LIMIT = 48 * 1024 * 1024
 
 
-FIRST = {"x": 2, "y_lo": 0, "core": 1, "z": 5, "y_hi": 2}
-
-
-def turned_range(axis):
-    return [(n + FIRST[axis]) % SIZES[axis] for n in range(SIZES[axis])]
+ORDER = {
+    "x": (2, 0, 1, 3),
+    "y_lo": (0, 1),
+    "core": (1, 0),
+    "z": (5, 6, 7, 0, 1, 2, 3, 4),
+    "y_hi": (2, 3, 0, 1),
+}
 
 
 def groups_over(axes):
@@ -31,7 +33,7 @@
     groups = []
     for fixed in itertools.product(*[range(SIZES[a]) for a in rest]):
         group = []
-        for moving in itertools.product(*[turned_range(a) for a in axes]):
+        for moving in itertools.product(*[ORDER[a] for a in axes]):
             place = dict(zip(rest, fixed)) | dict(zip(axes, moving))
             flat = 0
             for a in SIZES:
@@ -42,7 +44,7 @@
 
 
 SLOT = [0] * NBLK
-for place, (z, y) in enumerate(itertools.product(turned_range("z"), turned_range("y_hi"))):
+for place, (z, y) in enumerate(itertools.product(ORDER["z"], ORDER["y_hi"])):
     SLOT[z * SIZES["y_hi"] + y] = place
 
 PLANE_GROUPS = groups_over(("core", "z", "y_hi", "y_lo"))
@@ -74,6 +76,10 @@
     row = lax.broadcasted_iota(jnp.int32, (BLK, BLK), 0)
     col = lax.broadcasted_iota(jnp.int32, (BLK, BLK), 1)
     return jnp.where(col == source_of(row), 1.0, 0.0).astype(BF16)
+
+
+def one_hot(rows, cols, source_of):
+    return (np.arange(cols)[None, :] == source_of(np.arange(rows))[:, None]).astype(ml_dtypes.bfloat16)
 
 
 def pack_kernel(in_hbm, grad_hbm, out_ref, held, sems):
@@ -95,12 +101,13 @@
         out_ref[part * BLK : (part + 1) * BLK, :] = dot(perm, jnp.concatenate(pieces, axis=0)).astype(BF16)
 
 
-def correlate_kernel(rows_ref, forward_ref, back_ref, out_ref, xa, xb, xc, ga, gb, gc, zed, ybuf):
-    def source(m):
-        a, th, j8, core, y, c = m >> 7, (m >> 6) & 1, (m >> 3) & 7, (m >> 2) & 1, (m >> 1) & 1, m & 1
-        return core * 128 + (j8 * 2 + y) * 8 + a * 4 + c * 2 + th
-
-    perm = permutation(source)
+def correlate_source(m):
+    a, th, j8, core, y, c = m >> 7, (m >> 6) & 1, (m >> 3) & 7, (m >> 2) & 1, (m >> 1) & 1, m & 1
+    return core * 128 + (j8 * 2 + y) * 8 + a * 4 + c * 2 + th
+
+
+def correlate_kernel(rows_ref, perm_ref, forward_ref, back_ref, out_ref, xa, xb, xc, ga, gb, gc, zed, ybuf):
+    perm = perm_ref[...]
     blocks = [[], []]
     for part in range(4):
         both = [rows_ref[core * 512 + part * LANES : core * 512 + (part + 1) * LANES, :] for core in range(2)]
@@ -165,18 +172,23 @@
         out_ref[x * LANES : (x + 1) * LANES, :] = y
 
 
-def total_kernel(parts_ref, out_ref):
+def total_source(m):
+    return ((m >> 3) & 31) * 4 + (m & 3)
+
+
+def total_kernel(parts_ref, repeat_ref, out_ref):
     total = parts_ref[0:LANES].astype(F32)
     for n in range(1, 4):
         total = total + parts_ref[n * LANES : (n + 1) * LANES].astype(F32)
-    row = lax.broadcasted_iota(jnp.int32, (512, LANES), 0)
-    col = lax.broadcasted_iota(jnp.int32, (512, LANES), 1)
-    repeat = jnp.where(col == ((row >> 3) & 31) * 4 + (row & 3), 1.0, 0.0).astype(BF16)
-    out_ref[...] = dot(repeat, total.astype(BF16)).astype(BF16)
-
-
-def unpack_kernel(rows_ref, out_hbm, held, sems):
-    perm = permutation(lambda m: (m & 63) * 4 + (m >> 6))
+    out_ref[...] = dot(repeat_ref[...], total.astype(BF16)).astype(BF16)
+
+
+def unpack_source(m):
+    return (m & 63) * 4 + (m >> 6)
+
+
+def unpack_kernel(rows_ref, perm_ref, out_hbm, held, sems):
+    perm = perm_ref[...]
     halves = [dot(perm, rows_ref[part * BLK : (part + 1) * BLK, :]) for part in range(2)]
     copies = []
     for lh in range(2):
@@ -209,22 +221,22 @@
     correlate_kernel,
     (512, LANES),
     BF16,
-    [VMEM] * 3,
+    [VMEM] * 4,
     VMEM,
     [VMEM((2, BLK, LANES), F32)] * 6 + [VMEM((4, 64, LANES), F32), VMEM((LANES, LANES), F32)],
 )
-TOTAL = call(total_kernel, (512, LANES), BF16, [VMEM], VMEM)
-UNPACK = call(unpack_kernel, (BLK, BLK), F32, [VMEM], HBM, [VMEM((BLK, BLK), F32), TWO_SEMS])
+TOTAL = call(total_kernel, (512, LANES), BF16, [VMEM] * 2, VMEM)
+UNPACK = call(unpack_kernel, (BLK, BLK), F32, [VMEM] * 2, HBM, [VMEM((BLK, BLK), F32), TWO_SEMS])
 
 
 def on_device(inputs, out_grads):
     rows = PACK(*[pltpu.with_memory_space_constraint(a[0], HBM) for a in (inputs, out_grads)])
     rows = exchange(rows, PLANE_GROUPS)
-    parts = CORRELATE(rows, *make_tables())
+    parts = CORRELATE(rows, one_hot(BLK, BLK, correlate_source), *make_tables())
     parts = exchange(parts, X_GROUPS)
-    rows = TOTAL(parts)
+    rows = TOTAL(parts, one_hot(512, LANES, total_source))
     rows = exchange(rows, PLANE_GROUPS)
-    return UNPACK(rows)
+    return UNPACK(rows, one_hot(BLK, BLK, unpack_source))
 
 
 def solution(mesh):

time: 57.3 us -> 57.3 us (level)
  no operation moved by 1% of the time
where the time goes in v7:
time: 57.3 us; the launch traced here: 57.1 us
  blocking collectives  52.9 us (92%)
  Pallas kernels  4.12 us (7%)
    all_to_all x3, blocking collectives, exchange(): lax.all_to_all(rows, ('dp', 'ctx'), 0, 0, axis_index_groups=groups, tiled...  52.9 us
    pallas_call x1, Pallas kernels, on_device(): parts = CORRELATE(rows, one_hot(BLK, BLK, correlate_source), *make_tables())  1.56 us
    pallas_call x1, Pallas kernels, on_device(): PACK(*[pltpu.with_memory_space_constraint(a[0], HBM) for a in (inputs, ou...  1.39 us

profile of v7, /device:TPU:1, one launch (start us, length us, event | category | flops | bytes accessed | tf_op | source)
XLA Modules:
  0.0 57.1 jit_solution(8358925006431929101)
XLA Ops:
  0.0 0.0 copy-start.4
  0.0 1.4 %shard_map.73 = bf16[1024,128]{1,0:T(8,128)(2,1)S(1)} custom-call(bf16[256,256]{1,0:T(8,128)(2,1)} %bitcast.14, bf16[256,256]{1,0:T(8,128)(2,1)} %bitcast.15), custom_call_target="tpu_custom_call" | custom-call | tf_op jit(solution)/shard_map/pallas_call | solution.py:233
  1.4 0.0 copy-start
  1.4 0.0 copy-start.1
  1.4 27.7 %all_to_all.33 = bf16[128,8,128]{2,1,0:T(8,128)(2,1)S(1)} all-to-all(bf16[128,8,128]{2,1,0:T(8,128)(2,1)S(1)} %bitcast.8), channel_id=1, replica_groups={{54,118,55,119,52,116,53,117,58,122,59,123,56,120,57,121,62,126,63,127,..., dimensions={0} | all-to-all | bytes 524288 | tf_op jit(solution)/shard_map/all_to_all | solution.py:55
  29.1 0.0 copy-done.4
  29.1 0.0 copy-done
  29.1 0.0 copy-done.1
  29.1 1.6 %shard_map.74 = bf16[512,128]{1,0:T(8,128)(2,1)S(1)} custom-call(bf16[1024,128]{1,0:T(8,128)(2,1)S(1)} %bitcast.9, bf16[256,256]{1,0:T(8,128)(2,1)S(1)} %copy-done.4, bf16[256,512]{1,0:T(8,128)(2,1)S(1)} %copy-done.1, bf16[512,256]{1,0:T(8,128)(2,1)S(1)} %copy-done), custom_call_target="tpu_custom_call" | custom-call | tf_op jit(solution)/shard_map/pallas_call | solution.py:235
  30.7 0.0 copy-start.2
  30.7 7.4 %all_to_all.34 = bf16[4,128,128]{2,1,0:T(8,128)(2,1)S(1)} all-to-all(bf16[4,128,128]{2,1,0:T(8,128)(2,1)S(1)} %bitcast.13), channel_id=1, replica_groups={{256,0,128,384},{257,1,129,385},{258,2,130,386},{259,3,131,387},{260,4,..., dimensions={0} | all-to-all | bytes 262144 | tf_op jit(solution)/shard_map/all_to_all | solution.py:55
  38.2 0.0 copy-done.2
  38.2 0.2 shard_map.75
  38.3 0.0 copy-start.3
  38.4 17.7 %all_to_all.35 = bf16[128,4,128]{2,1,0:T(4,128)(2,1)S(1)} all-to-all(bf16[128,4,128]{2,1,0:T(4,128)(2,1)S(1)} %bitcast.11), channel_id=1, replica_groups={{54,118,55,119,52,116,53,117,58,122,59,123,56,120,57,121,62,126,63,127,..., dimensions={0} | all-to-all | bytes 262144 | tf_op jit(solution)/shard_map/all_to_all | solution.py:55
  56.1 0.0 copy-done.3
  56.1 1.0 %shard_map.76 = f32[256,256]{1,0:T(8,128)} custom-call(bf16[512,128]{1,0:T(8,128)(2,1)S(1)} %bitcast.12, bf16[256,256]{1,0:T(8,128)(2,1)S(1)} %copy-done.3), custom_call_target="tpu_custom_call" | custom-call | tf_op jit(solution)/shard_map/pallas_call | solution.py:239
Async XLA Ops:
  0.0 29.1 %copy-start.4 = (bf16[256,256]{1,0:T(8,128)(2,1)S(1)}, bf16[256,256]{1,0:T(8,128)(2,1)}, u32[]{:S(2)}) copy-start(bf16[256,256]{1,0:T(8,128)(2,1)} %constant.10.clone.perm_ref) | copy-start | bytes 393220
  1.4 27.7 %copy-start = (bf16[512,256]{1,0:T(8,128)(2,1)S(1)}, bf16[512,256]{1,0:T(8,128)(2,1)}, u32[]{:S(2)}) copy-start(bf16[512,256]{1,0:T(8,128)(2,1)} %constant.12.clone.back_ref) | copy-start | bytes 786436
  1.4 27.7 %copy-start.1 = (bf16[256,512]{1,0:T(8,128)(2,1)S(1)}, bf16[256,512]{1,0:T(8,128)(2,1)}, u32[]{:S(2)}) copy-start(bf16[256,512]{1,0:T(8,128)(2,1)} %constant.11.clone.forward_ref) | copy-start | bytes 786436
  30.7 7.5 %copy-start.2 = (bf16[512,128]{1,0:T(8,128)(2,1)S(1)}, bf16[512,128]{1,0:T(8,128)(2,1)}, u32[]{:S(2)}) copy-start(bf16[512,128]{1,0:T(8,128)(2,1)} %constant.13.clone.repeat_ref) | copy-start | bytes 393220
  38.3 17.8 %copy-start.3 = (bf16[256,256]{1,0:T(8,128)(2,1)S(1)}, bf16[256,256]{1,0:T(8,128)(2,1)}, u32[]{:S(2)}) copy-start(bf16[256,256]{1,0:T(8,128)(2,1)} %constant.14.clone.perm_ref) | copy-start | bytes 393220

commit v8 on v7

--- a/solution.py
+++ b/solution.py
@@ -184,19 +184,16 @@
 
 
 def unpack_source(m):
-    return (m & 63) * 4 + (m >> 6)
-
-
-def unpack_kernel(rows_ref, perm_ref, out_hbm, held, sems):
-    perm = perm_ref[...]
-    halves = [dot(perm, rows_ref[part * BLK : (part + 1) * BLK, :]) for part in range(2)]
+    return (m & 127) * 4 + ((m >> 7) & 1) * 2 + (m >> 8)
+
+
+def unpack_kernel(rows_ref, pick_ref, out_hbm, held, sems):
+    received = rows_ref[...]
     copies = []
     for lh in range(2):
         rows = slice(lh * LANES, (lh + 1) * LANES)
-        for c in range(2):
-            at = (c * 2 + lh) * 64
-            block = jnp.concatenate([halves[part][at : at + 64] for part in range(2)], axis=0)
-            held[rows, c * LANES : (c + 1) * LANES] = jnp.transpose(block)
+        pick = pick_ref[:, lh * BLK : (lh + 1) * BLK]
+        held[rows, :] = lax.dot_general(received, pick, (((0,), (0,)), ((), ())), preferred_element_type=F32)
         copies.append(pltpu.make_async_copy(held.at[rows], out_hbm.at[rows], sems.at[lh]))
         copies[-1].start()
     for copy in copies:
@@ -236,7 +233,7 @@
     parts = exchange(parts, X_GROUPS)
     rows = TOTAL(parts, one_hot(512, LANES, total_source))
     rows = exchange(rows, PLANE_GROUPS)
-    return UNPACK(rows, one_hot(BLK, BLK, unpack_source))
+    return UNPACK(rows, one_hot(512, 512, unpack_source).T)
 
 
 def solution(mesh):

time: 57.3 us -> 57.2 us (level)
  no operation moved by 1% of the time
where the time goes in v8:
time: 57.2 us; the launch traced here: 56.9 us
  blocking collectives  52.7 us (92%)
  Pallas kernels  4.09 us (7%)
    all_to_all x3, blocking collectives, exchange(): lax.all_to_all(rows, ('dp', 'ctx'), 0, 0, axis_index_groups=groups, tiled...  52.7 us
    pallas_call x1, Pallas kernels, on_device(): parts = CORRELATE(rows, one_hot(BLK, BLK, correlate_source), *make_tables())  1.56 us
    pallas_call x1, Pallas kernels, on_device(): PACK(*[pltpu.with_memory_space_constraint(a[0], HBM) for a in (inputs, ou...  1.39 us

profile of v8, /device:TPU:1, one launch (start us, length us, event | category | flops | bytes accessed | tf_op | source)
XLA Modules:
  0.0 56.9 jit_solution(4824997292336300389)
XLA Ops:
  0.0 0.0 copy-start.4
  0.0 1.4 %shard_map.73 = bf16[1024,128]{1,0:T(8,128)(2,1)S(1)} custom-call(bf16[256,256]{1,0:T(8,128)(2,1)} %bitcast.14, bf16[256,256]{1,0:T(8,128)(2,1)} %bitcast.15), custom_call_target="tpu_custom_call" | custom-call | tf_op jit(solution)/shard_map/pallas_call | solution.py:230
  1.4 0.0 copy-start.1
  1.4 0.0 copy-start.2
  1.4 27.7 %all_to_all.33 = bf16[128,8,128]{2,1,0:T(8,128)(2,1)S(1)} all-to-all(bf16[128,8,128]{2,1,0:T(8,128)(2,1)S(1)} %bitcast.8), channel_id=1, replica_groups={{54,118,55,119,52,116,53,117,58,122,59,123,56,120,57,121,62,126,63,127,..., dimensions={0} | all-to-all | bytes 524288 | tf_op jit(solution)/shard_map/all_to_all | solution.py:55
  29.1 0.0 copy-done.4
  29.1 0.0 copy-done.1
  29.1 0.0 copy-done.2
  29.1 0.0 copy-start.3
  29.1 1.6 %shard_map.74 = bf16[512,128]{1,0:T(8,128)(2,1)S(1)} custom-call(bf16[1024,128]{1,0:T(8,128)(2,1)S(1)} %bitcast.9, bf16[256,256]{1,0:T(8,128)(2,1)S(1)} %copy-done.4, bf16[256,512]{1,0:T(8,128)(2,1)S(1)} %copy-done.2, bf16[512,256]{1,0:T(8,128)(2,1)S(1)} %copy-done.1), custom_call_target="tpu_custom_call" | custom-call | tf_op jit(solution)/shard_map/pallas_call | solution.py:232
  30.7 0.0 copy-start
  30.7 7.4 %all_to_all.34 = bf16[4,128,128]{2,1,0:T(8,128)(2,1)S(1)} all-to-all(bf16[4,128,128]{2,1,0:T(8,128)(2,1)S(1)} %bitcast.13), channel_id=1, replica_groups={{256,0,128,384},{257,1,129,385},{258,2,130,386},{259,3,131,387},{260,4,..., dimensions={0} | all-to-all | bytes 262144 | tf_op jit(solution)/shard_map/all_to_all | solution.py:55
  38.2 0.0 copy-done.3
  38.2 0.2 shard_map.75
  38.3 17.6 %all_to_all.35 = bf16[128,4,128]{2,1,0:T(4,128)(2,1)S(1)} all-to-all(bf16[128,4,128]{2,1,0:T(4,128)(2,1)S(1)} %bitcast.11), channel_id=1, replica_groups={{54,118,55,119,52,116,53,117,58,122,59,123,56,120,57,121,62,126,63,127,..., dimensions={0} | all-to-all | bytes 262144 | tf_op jit(solution)/shard_map/all_to_all | solution.py:55
  56.0 0.0 copy-done
  56.0 1.0 %shard_map.76 = f32[256,256]{1,0:T(8,128)} custom-call(bf16[512,128]{1,0:T(8,128)(2,1)S(1)} %bitcast.12, bf16[512,512]{1,0:T(8,128)(2,1)S(1)} %copy-done), custom_call_target="tpu_custom_call" | custom-call | tf_op jit(solution)/shard_map/pallas_call | solution.py:236
Async XLA Ops:
  0.0 29.1 %copy-start.4 = (bf16[256,256]{1,0:T(8,128)(2,1)S(1)}, bf16[256,256]{1,0:T(8,128)(2,1)}, u32[]{:S(2)}) copy-start(bf16[256,256]{1,0:T(8,128)(2,1)} %constant.10.clone.perm_ref) | copy-start | bytes 393220
  1.4 27.7 %copy-start.1 = (bf16[512,256]{1,0:T(8,128)(2,1)S(1)}, bf16[512,256]{1,0:T(8,128)(2,1)}, u32[]{:S(2)}) copy-start(bf16[512,256]{1,0:T(8,128)(2,1)} %constant.12.clone.back_ref) | copy-start | bytes 786436
  1.4 27.7 %copy-start.2 = (bf16[256,512]{1,0:T(8,128)(2,1)S(1)}, bf16[256,512]{1,0:T(8,128)(2,1)}, u32[]{:S(2)}) copy-start(bf16[256,512]{1,0:T(8,128)(2,1)} %constant.11.clone.forward_ref) | copy-start | bytes 786436
  29.1 9.0 %copy-start.3 = (bf16[512,128]{1,0:T(8,128)(2,1)S(1)}, bf16[512,128]{1,0:T(8,128)(2,1)}, u32[]{:S(2)}) copy-start(bf16[512,128]{1,0:T(8,128)(2,1)} %constant.13.clone.repeat_ref) | copy-start | bytes 393220
  30.7 25.3 %copy-start = (bf16[512,512]{1,0:T(8,128)(2,1)S(1)}, bf16[512,512]{1,0:T(8,128)(2,1)}, u32[]{:S(2)}) copy-start(bf16[512,512]{1,0:T(8,128)(2,1)} %constant.14.clone.pick_ref) | copy-start | bytes 1572868

commit v9 on v7

--- a/solution.py
+++ b/solution.py
@@ -23,7 +23,7 @@
     "x": (2, 0, 1, 3),
     "y_lo": (0, 1),
     "core": (1, 0),
-    "z": (5, 6, 7, 0, 1, 2, 3, 4),
+    "z": (6, 7, 0, 1, 2, 3, 4, 5),
     "y_hi": (2, 3, 0, 1),
 }
 

time: 57.3 us -> 57.3 us (level)
  no operation moved by 1% of the time
where the time goes in v9:
time: 57.3 us; the launch traced here: 57.1 us
  blocking collectives  52.9 us (92%)
  Pallas kernels  4.13 us (7%)
    all_to_all x3, blocking collectives, exchange(): lax.all_to_all(rows, ('dp', 'ctx'), 0, 0, axis_index_groups=groups, tiled...  52.9 us
    pallas_call x1, Pallas kernels, on_device(): parts = CORRELATE(rows, one_hot(BLK, BLK, correlate_source), *make_tables())  1.57 us
    pallas_call x1, Pallas kernels, on_device(): PACK(*[pltpu.with_memory_space_constraint(a[0], HBM) for a in (inputs, ou...  1.39 us

profile of v9, /device:TPU:1, one launch (start us, length us, event | category | flops | bytes accessed | tf_op | source)
XLA Modules:
  0.0 57.1 jit_solution(1898182384553345245)
XLA Ops:
  0.0 0.0 copy-start.4
  0.0 1.4 %shard_map.73 = bf16[1024,128]{1,0:T(8,128)(2,1)S(1)} custom-call(bf16[256,256]{1,0:T(8,128)(2,1)} %bitcast.14, bf16[256,256]{1,0:T(8,128)(2,1)} %bitcast.15), custom_call_target="tpu_custom_call" | custom-call | tf_op jit(solution)/shard_map/pallas_call | solution.py:233
  1.4 0.0 copy-start
  1.4 0.0 copy-start.1
  1.4 27.7 %all_to_all.33 = bf16[128,8,128]{2,1,0:T(8,128)(2,1)S(1)} all-to-all(bf16[128,8,128]{2,1,0:T(8,128)(2,1)S(1)} %bitcast.8), channel_id=1, replica_groups={{58,122,59,123,56,120,57,121,62,126,63,127,60,124,61,125,34,98,35,99,32..., dimensions={0} | all-to-all | bytes 524288 | tf_op jit(solution)/shard_map/all_to_all | solution.py:55
  29.2 0.0 copy-done.4
  29.2 0.0 copy-done
  29.2 0.0 copy-done.1
  29.2 1.6 %shard_map.74 = bf16[512,128]{1,0:T(8,128)(2,1)S(1)} custom-call(bf16[1024,128]{1,0:T(8,128)(2,1)S(1)} %bitcast.9, bf16[256,256]{1,0:T(8,128)(2,1)S(1)} %copy-done.4, bf16[256,512]{1,0:T(8,128)(2,1)S(1)} %copy-done.1, bf16[512,256]{1,0:T(8,128)(2,1)S(1)} %copy-done), custom_call_target="tpu_custom_call" | custom-call | tf_op jit(solution)/shard_map/pallas_call | solution.py:235
  30.8 0.0 copy-start.2
  30.8 7.4 %all_to_all.34 = bf16[4,128,128]{2,1,0:T(8,128)(2,1)S(1)} all-to-all(bf16[4,128,128]{2,1,0:T(8,128)(2,1)S(1)} %bitcast.13), channel_id=1, replica_groups={{256,0,128,384},{257,1,129,385},{258,2,130,386},{259,3,131,387},{260,4,..., dimensions={0} | all-to-all | bytes 262144 | tf_op jit(solution)/shard_map/all_to_all | solution.py:55
  38.2 0.0 copy-done.2
  38.2 0.2 shard_map.75
  38.4 0.0 copy-start.3
  38.4 17.7 %all_to_all.35 = bf16[128,4,128]{2,1,0:T(4,128)(2,1)S(1)} all-to-all(bf16[128,4,128]{2,1,0:T(4,128)(2,1)S(1)} %bitcast.11), channel_id=1, replica_groups={{58,122,59,123,56,120,57,121,62,126,63,127,60,124,61,125,34,98,35,99,32..., dimensions={0} | all-to-all | bytes 262144 | tf_op jit(solution)/shard_map/all_to_all | solution.py:55
  56.1 0.0 copy-done.3
  56.1 1.0 %shard_map.76 = f32[256,256]{1,0:T(8,128)} custom-call(bf16[512,128]{1,0:T(8,128)(2,1)S(1)} %bitcast.12, bf16[256,256]{1,0:T(8,128)(2,1)S(1)} %copy-done.3), custom_call_target="tpu_custom_call" | custom-call | tf_op jit(solution)/shard_map/pallas_call | solution.py:239
Async XLA Ops:
  0.0 29.2 %copy-start.4 = (bf16[256,256]{1,0:T(8,128)(2,1)S(1)}, bf16[256,256]{1,0:T(8,128)(2,1)}, u32[]{:S(2)}) copy-start(bf16[256,256]{1,0:T(8,128)(2,1)} %constant.10.clone.perm_ref) | copy-start | bytes 393220
  1.4 27.8 %copy-start = (bf16[512,256]{1,0:T(8,128)(2,1)S(1)}, bf16[512,256]{1,0:T(8,128)(2,1)}, u32[]{:S(2)}) copy-start(bf16[512,256]{1,0:T(8,128)(2,1)} %constant.12.clone.back_ref) | copy-start | bytes 786436
  1.4 27.8 %copy-start.1 = (bf16[256,512]{1,0:T(8,128)(2,1)S(1)}, bf16[256,512]{1,0:T(8,128)(2,1)}, u32[]{:S(2)}) copy-start(bf16[256,512]{1,0:T(8,128)(2,1)} %constant.11.clone.forward_ref) | copy-start | bytes 786436
  30.8 7.5 %copy-start.2 = (bf16[512,128]{1,0:T(8,128)(2,1)S(1)}, bf16[512,128]{1,0:T(8,128)(2,1)}, u32[]{:S(2)}) copy-start(bf16[512,128]{1,0:T(8,128)(2,1)} %constant.13.clone.repeat_ref) | copy-start | bytes 393220
  38.4 17.7 %copy-start.3 = (bf16[256,256]{1,0:T(8,128)(2,1)S(1)}, bf16[256,256]{1,0:T(8,128)(2,1)}, u32[]{:S(2)}) copy-start(bf16[256,256]{1,0:T(8,128)(2,1)} %constant.14.clone.perm_ref) | copy-start | bytes 393220
